TPU v7x, 32 devices: a whole 2x2x4 slice. The times are simulated.
32 devices in a mesh: row: 2 (over core), sector: 4 (over y, x), inst: 4 (over z).
Axes of the slice: x: 2, y: 2, z: 4, core: 2. Of those that a mesh axis runs over, the one named last changes fastest.
Arguments:
- state: bfloat16 [2, 4, 8, 5, 16384], P('row', 'sector', 'inst'), may hold values from -6 to 6
- gradients: bfloat16 [2, 4, 8, 15, 16384], P('row', 'sector', 'inst'), may hold values from -6 to 6
- jacobian: bfloat16 [2, 4, 8, 25, 16384], P('row', 'sector', 'inst'), may hold values from -2.5 to 2.5
- pseudo_step: float32 [2, 4, 8, 16384], P('row', 'sector', 'inst'), may hold values from 0.25 to 0.6
- frequency: float32 [2], P('row'), may hold values from 0.1 to 0.4
- donor_cells: int32 [2, 4, 8, 128], P('row', 'sector'), may hold values from 0 to 16383
- block_count: int32 [2, 4], P('row', 'sector'), may hold values from 2 to 8, as said below
- matching: int32 [2, 4, 8, 8], P('row', 'sector', 'inst'), may hold values from 0 to 3, as said below
- target_cells: int32 [2, 4, 8, 4, 2, 128], P('row', 'sector', 'inst'), may hold values from 0 to 16383
- interp_weights: bfloat16 [2, 4, 8, 4, 2, 128, 128], P('row', 'sector', 'inst'), may hold values from -0.5 to 0.5
- face_offsets: float32 [2, 4, 8, 4, 2, 3, 128], P('row', 'sector', 'inst'), may hold values from -3 to 3
Outputs:
- updated: float32 [2, 4, 8, 5, 16384], P('row', 'sector', 'inst')
Inputs may be any that keep to these rules, and one draw needn't show every extreme that they name: `block_count`: every row has a sector with exactly 8 live blocks; live blocks of a sector are its first ones. `matching`: among the live blocks of one sector and instance, at most 2 name the same receiving sector; for every donor row and instance some receiving sector is named by exactly 2 live blocks of every donor sector.
All inputs are finite; a program needn't handle non-finite values.
Results may differ from a plain program's by a relative error of at most 0.0029.
Values may be sent and summed in bfloat16 or wider, within the bound.
A program may use at most 128 MiB of HBM per device.

v0:
```python
import math

import jax
import jax.numpy as jnp
from jax import lax
from jax.sharding import PartitionSpec as P

SWEEPS = 6


def swapped(value, axis, bit):
    mask = 2**bit
    pairs = [(source, source ^ mask) for source in range(lax.axis_size(axis))]
    return lax.ppermute(value, axis, pairs)


def spectral_block(row_first, row_count, col_count, period):
    row_index = row_first + jnp.arange(row_count, dtype=jnp.int32)[:, None]
    col_index = jnp.arange(col_count, dtype=jnp.int32)[None, :]
    index_gap = row_index - col_index
    diagonal_mask = index_gap == 0
    safe_gap = jnp.where(diagonal_mask, 1, index_gap)
    phase_angle = safe_gap.astype(jnp.float32) * (math.pi / period)
    sign_flip = (1 - 2 * (jnp.abs(index_gap) % 2)).astype(jnp.float32)
    cot_entry = 0.5 * sign_flip * jnp.cos(phase_angle) / jnp.sin(phase_angle)
    return jnp.where(diagonal_mask, jnp.zeros_like(cot_entry), cot_entry)


def slot_ranks(receiver, is_live, sectors):
    one_hot = (receiver[..., None] == jnp.arange(sectors, dtype=jnp.int32)).astype(jnp.int32)
    one_hot = one_hot * is_live[..., None].astype(jnp.int32)
    earlier = jnp.cumsum(one_hot, axis=-2) - one_hot
    return jnp.sum(earlier * one_hot, axis=-1)


def couple_faces(mixed, offsets, nvar):
    face_values = mixed[..., :nvar, :]
    face_slopes = mixed[..., nvar:, :].reshape(mixed.shape[:-2] + (3, nvar, mixed.shape[-1]))
    return face_values + jnp.sum(offsets[..., :, None, :] * face_slopes, axis=-3)


def apply_jacobian(jacobi_wide, vector):
    return jnp.sum(jacobi_wide.astype(jnp.float32) * vector[:, None], axis=2)


def body(
    state,
    gradients,
    jacobian,
    pseudo_step,
    frequency,
    donor_cells,
    block_count,
    matching,
    target_cells,
    interp_weights,
    face_offsets,
):
    flow = state[0, 0]
    slopes = gradients[0, 0]
    jacobi = jacobian[0, 0]
    pseudo = pseudo_step[0, 0]
    rotation = frequency[0]
    face_cells = donor_cells[0, 0]
    live_count = block_count[0, 0]
    receiver = matching[0, 0]
    targets = target_cells[0, 0]
    weights = interp_weights[0, 0]
    offsets = face_offsets[0, 0]
    inst_local, nvar, cell_count = flow.shape
    block_slots, face_width = face_cells.shape
    sectors = lax.axis_size("sector")
    capacity = targets.shape[2]
    stacked = jnp.concatenate([flow, slopes], axis=1)
    frow_count = stacked.shape[1]
    face_rows = jnp.take(stacked, face_cells.reshape(-1), axis=2).reshape(
        inst_local, frow_count, block_slots, face_width
    )
    partner = swapped((face_rows[None], receiver[None], live_count.reshape(1)), "row", 0)
    all_faces, all_receiver, all_count = (
        lax.all_gather(partner[0], "sector", axis=0, tiled=True),
        lax.all_gather(partner[1], "sector", axis=0, tiled=True),
        lax.all_gather(partner[2], "sector", axis=0, tiled=True),
    )
    is_live = jnp.arange(block_slots, dtype=jnp.int32)[None, None, :] < all_count[:, None, None]
    is_live = jnp.broadcast_to(is_live, all_receiver.shape)
    slot_rank = slot_ranks(all_receiver, is_live, sectors)
    wanted = is_live & (all_receiver == lax.axis_index("sector"))
    rank_match = (
        slot_rank[:, :, None, :] == jnp.arange(capacity, dtype=jnp.int32)[None, None, :, None]
    )
    selector = (wanted[:, :, None, :] & rank_match).astype(jnp.bfloat16)
    arrived = jnp.einsum(
        "stkb,stqbf->tskqf", selector, all_faces, preferred_element_type=jnp.float32
    ).astype(jnp.bfloat16)
    mixed = jnp.einsum("tskqf,tskfg->tskqg", arrived, weights, preferred_element_type=jnp.float32)
    coupled = couple_faces(mixed, offsets, nvar)

    def spread_faces(faces_one, targets_one):
        flat_faces = faces_one.transpose(2, 0, 1, 3).reshape(nvar, -1)
        return (
            jnp.zeros((nvar, cell_count), jnp.float32)
            .at[:, targets_one.reshape(-1)]
            .add(flat_faces)
        )

    coupling = jax.vmap(spread_faces)(coupled, targets)
    first_row = lax.axis_index("inst") * inst_local
    period = inst_local * lax.axis_size("inst")
    segment = lax.all_gather(flow, "inst", axis=0, tiled=True)
    block_rows = spectral_block(first_row, inst_local, segment.shape[0], period)
    spectral = jnp.einsum(
        "tu,uvc->tvc", block_rows, segment.astype(jnp.float32), precision=lax.Precision.HIGHEST
    )
    flow_wide = flow.astype(jnp.float32)
    jacobi_wide = jacobi.reshape(inst_local, nvar, nvar, cell_count)
    residual = apply_jacobian(jacobi_wide, flow_wide) + rotation * spectral - coupling
    increment = -pseudo[:, None, :] * residual
    for sweep in range(SWEEPS):
        increment = -pseudo[:, None, :] * (residual + apply_jacobian(jacobi_wide, increment))
    return (flow_wide + increment)[None, None]


def solution(mesh):
    placed = (
        P("row", "sector", "inst", None, None),
        P("row", "sector", "inst", None, None),
        P("row", "sector", "inst", None, None),
        P("row", "sector", "inst", None),
        P("row"),
        P("row", "sector", None, None),
        P("row", "sector"),
        P("row", "sector", "inst", None),
        P("row", "sector", "inst", None, None, None),
        P("row", "sector", "inst", None, None, None, None),
        P("row", "sector", "inst", None, None, None, None),
    )
    return jax.shard_map(
        body,
        mesh=mesh,
        in_specs=placed,
        out_specs=P("row", "sector", "inst", None, None),
        check_vma=False,
    )
```

profile of v0, /device:TPU:0, one launch (start us, length us, event | category | flops | bytes accessed | tf_op | source)
XLA Modules:
  0.0 123.0 jit_solution(4243604905876143394)
XLA Ops:
  6.5 0.5 collective-permute-start
  7.0 0.1 collective-permute-start.1
  7.1 3.0 %pad_maximum_fusion = bf16[2,20,16384]{2,0,1:T(2,128)(2,1)S(1)} fusion(bf16[2,15,16384]{2,0,1:T(2,128)(2,1)} %bitcast.68, bf16[2,5,16384]{2,0,1:T(2,128)(2,1)} %bitcast.66), kind=kLoop, calls=%fused_computation.21 | loop fusion | flops 655360 | bytes 2621440 | tf_op jit(solution)/shard_map/concatenate | solution.py:74
  10.0 0.0 copy-start.5
  10.0 0.0 copy-start.2
  10.0 13.1 %copy.36 = bf16[2,20,16384]{1,0,2:T(2,128)(2,1)} copy(bf16[2,20,16384]{2,0,1:T(2,128)(2,1)S(1)} %pad_maximum_fusion) | data formatting | bytes 2621440 | tf_op jit(solution)/shard_map/concatenate | solution.py:74
  23.1 0.0 copy-start.3
  23.2 0.0 copy-start.9
  23.2 0.0 copy-start.1
  23.2 7.2 %gather_fusion = bf16[1024,2,20]{2,1,0:T(2,128)(2,1)S(1)} fusion(bf16[2,20,16384]{1,0,2:T(2,128)(2,1)} %copy.36, s32[1024]{0:T(1024)S(1)} %broadcast_clamp_fusion), kind=kCustom, calls=%fused_computation | custom fusion | bytes 167936 | tf_op jit(solution)/shard_map/jit(_take)/gather | solution.py:76
  30.4 0.3 copy.37
  30.7 0.5 collective-permute-start.2
  31.2 1.0 copy.32
  32.2 0.0 all-gather.3.cloned.1.call-update
  32.2 0.0 copy-start.4
  32.3 0.2 bitcast_convert_fusion
  32.6 0.1 multiply_reduce_fusion.1
  32.7 0.1 and_reduce_fusion
  32.8 0.1 negate_bitcast_fusion
  32.9 0.7 dynamic-slice
  33.6 2.8 %fusion.4 = f32[2,5,16384]{2,0,1:T(2,128)} fusion(bf16[2,5,5,16384]{3,0,2,1:T(2,128)(2,1)S(1)} %bitcast.58, f32[2,5,16384]{2,0,1:T(2,128)S(1)} %bitcast_convert_fusion), kind=kLoop, calls=%fused_computation.14 | loop fusion | flops 2293760 | bytes 2949120 | tf_op jit(solution)/shard_map/reduce_sum | solution.py:43
  36.4 1.4 %dynamic-update-slice = s32[4]{0:T(128)S(1)} dynamic-update-slice(s32[4]{0:T(128)S(1)} %broadcast.191, s32[1]{0:T(128)} %collective-permute-done, u32[]{:T(128)} %bitcast.7) | dynamic-update-slice | bytes 12
  38.5 8.4 %all-reduce = s32[4]{0:T(128)S(1)} all-reduce(s32[4]{0:T(128)S(1)} %dynamic-update-slice), channel_id=1, replica_groups=mesh['row'=2,'sector'=4,'inst'=4] {'sector'}, use_global_device_ids=true, to_apply=%add | all-reduce | flops 4 | bytes 32
  46.9 0.1 fusion.57
  47.0 8.0 %all_gather.14 = s32[4,2,8]{2,1,0:T(2,128)S(1)} all-gather(s32[1,2,8]{2,1,0:T(2,128)S(1)} %collective-permute-done.1), channel_id=1, replica_groups=mesh['row'=2,'sector'=4,'inst'=4] {'sector'}, dimensions={0}, use_global_device_ids=true | all-gather | bytes 320 | tf_op jit(solution)/shard_map/all_gather | solution.py:82
  55.0 1.4 %reduce_window_sum.11 = s32[4,2,8,4]{2,3,1,0:T(4,128)S(1)} reduce-window(s32[4,2,8,4]{2,3,1,0:T(4,128)S(1)} %fusion.19, s32[]{:T(128)} %constant.30.clone.1), window={size=1x1x8x1 pad=0_0x0_0x7_0x0_0}, to_apply=%region_1.2 | reduce-window | flops 1792 | bytes 2052 | tf_op jit(solution)/shard_map/jit(cumsum)/reduce_window_sum | solution.py:32
  56.5 8.6 %all_gather.15 = bf16[4,2,20,8,128]{4,3,2,1,0:T(8,128)(2,1)S(1)} all-gather(bf16[1,2,20,8,128]{4,3,2,1,0:T(8,128)(2,1)} %collective-permute-done.2), channel_id=1, replica_groups=mesh['row'=2,'sector'=4,'inst'=4] {'sector'}, dimensions={0}, use_global_device_ids=true | all-gather | bytes 409600 | tf_op jit(solution)/shard_map/all_gather | solution.py:81
  65.1 0.2 convolution_convert_fusion
  65.4 0.3 fusion.13
  65.7 0.1 copy.40
  65.7 0.1 multiply_reduce_fusion
  65.9 1.4 %copy.46 = f32[2,1024,5]{2,1,0:T(8,128)} copy(f32[2,1024,5]{1,0,2:T(2,128)S(1)} %bitcast.71) | data formatting | bytes 81920 | tf_op jit(solution)/shard_map/vmap()/reshape | solution.py:100
  67.3 18.6 %scatter_custom_fusion = f32[5,32768]{0,1:T(8,128)} fusion(s32[2048]{0:T(1024)S(1)} %bitcast.75, f32[2048,5]{1,0:T(8,128)} %bitcast.67, f32[]{:T(128)} %constant.20.clone.1), kind=kCustom, calls=%fused_computation.5 | custom fusion | flops 10240 | bytes 655872
  85.9 10.0 %copy.47 = f32[5,2,16384]{2,1,0:T(2,128)S(1)} copy(f32[5,2,16384]{0,2,1:T(8,128)} %bitcast.65) | data formatting | bytes 1310720
  95.8 0.0 all-gather.3.cloned.1.call-done
  95.9 4.6 %broadcast_multiply_fusion = (f32[2,5,16384]{2,0,1:T(2,128)S(1)}, f32[2,5,16384]{2,0,1:T(2,128)S(1)}) fusion(f32[2,16384]{1,0:T(2,128)S(1)} %negate_bitcast_fusion, f32[5,2,16384]{2,1,0:T(2,128)S(1)} %copy.47, f32[2,5,16384]{2,0,1:T(2,128)} %fusion.4, bf16[1,1,8,5,16384]{4,3,1,0,2:T(8,128)(2,1)} %all-gather.3.cloned.1.call-done, s32[2]{0:T(128)S(1)} %iota_add_fusion, ...), kind=kOutput, calls=%fused_computation.34 | convolution fusion | flops 16384384 | bytes 4063244 | tf_op jit(solution)/shard_map/tu,uvc->tvc/dot_general | solution.py:112
  100.5 2.0 %fusion.5 = f32[2,5,16384]{2,0,1:T(2,128)S(1)} fusion(bf16[2,5,5,16384]{3,0,2,1:T(2,128)(2,1)S(1)} %bitcast.59, f32[2,5,16384]{2,0,1:T(2,128)S(1)} %get-tuple-element.7), kind=kLoop, calls=%fused_computation.15 | loop fusion | flops 2293760 | bytes 2949120 | tf_op jit(solution)/shard_map/reduce_sum | solution.py:43
  102.6 0.4 add_multiply_fusion.4
  102.9 2.0 %fusion.6 = f32[2,5,16384]{2,0,1:T(2,128)S(1)} fusion(bf16[2,5,5,16384]{3,0,2,1:T(2,128)(2,1)S(1)} %bitcast.60, f32[2,5,16384]{2,0,1:T(2,128)S(1)} %add_multiply_fusion.4), kind=kLoop, calls=%fused_computation.16 | loop fusion | flops 2293760 | bytes 2949120 | tf_op jit(solution)/shard_map/reduce_sum | solution.py:43
  105.0 0.4 add_multiply_fusion.3
  105.3 2.0 %fusion.7 = f32[2,5,16384]{2,0,1:T(2,128)S(1)} fusion(bf16[2,5,5,16384]{3,0,2,1:T(2,128)(2,1)S(1)} %bitcast.61, f32[2,5,16384]{2,0,1:T(2,128)S(1)} %add_multiply_fusion.3), kind=kLoop, calls=%fused_computation.17 | loop fusion | flops 2293760 | bytes 2949120 | tf_op jit(solution)/shard_map/reduce_sum | solution.py:43
  107.4 0.4 add_multiply_fusion.2
  107.7 2.2 %fusion.8 = f32[2,5,16384]{2,0,1:T(2,128)S(1)} fusion(bf16[2,5,5,16384]{3,0,2,1:T(2,128)(2,1)S(1)} %bitcast.62, f32[2,5,16384]{2,0,1:T(2,128)S(1)} %add_multiply_fusion.2), kind=kLoop, calls=%fused_computation.18 | loop fusion | flops 2293760 | bytes 2949120 | tf_op jit(solution)/shard_map/reduce_sum | solution.py:43
  110.0 0.4 add_multiply_fusion.1
  110.4 2.0 %fusion.9 = f32[2,5,16384]{2,0,1:T(2,128)S(1)} fusion(bf16[2,5,5,16384]{3,0,2,1:T(2,128)(2,1)S(1)} %bitcast.63, f32[2,5,16384]{2,0,1:T(2,128)S(1)} %add_multiply_fusion.1), kind=kLoop, calls=%fused_computation.19 | loop fusion | flops 2293760 | bytes 2949120 | tf_op jit(solution)/shard_map/reduce_sum | solution.py:43
  112.4 0.4 add_multiply_fusion
  112.8 2.0 %fusion.10 = f32[2,5,16384]{2,0,1:T(2,128)S(1)} fusion(bf16[2,5,5,16384]{3,0,2,1:T(2,128)(2,1)S(1)} %bitcast.64, f32[2,5,16384]{2,0,1:T(2,128)S(1)} %add_multiply_fusion), kind=kLoop, calls=%fused_computation.20 | loop fusion | flops 2293760 | bytes 2949120 | tf_op jit(solution)/shard_map/reduce_sum | solution.py:43
  114.8 1.3 %add_bitcast_fusion = f32[1,1,2,5,16384]{4,2,3,1,0:T(2,128)} fusion(f32[2,5,16384]{2,0,1:T(2,128)S(1)} %get-tuple-element.8, f32[2,5,16384]{2,0,1:T(2,128)S(1)} %fusion.10, f32[2,16384]{1,0:T(2,128)S(1)} %negate_bitcast_fusion, bf16[1,1,2,5,16384]{4,2,3,1,0:T(2,128)(2,1)S(1)} %copy-done.2), kind=kLoop, calls=%fused_computation.25 | loop fusion | flops 655360 | bytes 2424832 | tf_op jit(solution)/shard_map/broadcast_in_dim | solution.py:121
  (38 shorter events, 0.3 us)
Async XLA Ops:
  6.5 58.8 %copy-start = (bf16[1,1,2,4,2,128,128]{6,5,4,3,2,1,0:T(8,128)(2,1)S(1)}, bf16[1,1,2,4,2,128,128]{6,5,4,3,2,1,0:T(8,128)(2,1)}, u32[]{:S(2)}) copy-start(bf16[1,1,2,4,2,128,128]{6,5,4,3,2,1,0:T(8,128)(2,1)} %param.20) | copy-start | bytes 1572868
  6.5 89.3 %all-gather.3.cloned.1.call-start = ((), (), s32[]{:S(2)}) async-start(), calls=%async_computation | async-start | bytes 2621440 | tf_op jit(solution)/shard_map/all_gather | solution.py:110
  6.5 29.9 %collective-permute-start = (s32[1]{0:T(128)}, s32[1]{0:T(128)}, u32[]{:S(2)}, u32[]{:S(2)}) collective-permute-start(s32[1]{0:T(128)} %bitcast.6), channel_id=1, source_target_pairs={{0,16},{16,0},{1,17},{17,1},{2,18},{18,2},{3,19},{19,3},{4,20},{20... | collective-permute-start | bytes 20 | tf_op jit(solution)/shard_map/ppermute | solution.py:14
  7.0 40.0 %collective-permute-start.1 = (s32[1,2,8]{2,1,0:T(2,128)}, s32[1,2,8]{2,1,0:T(2,128)S(1)}, u32[]{:S(2)}, u32[]{:S(2)}) collective-permute-start(s32[1,2,8]{2,1,0:T(2,128)} %bitcast.76), channel_id=1, source_target_pairs={{0,16},{16,0},{1,17},{17,1},{2,18},{18,2},{3,19},{19,3},{4,20},{20... | collective-permute-start | bytes 200 | tf_op jit(solution)/shard_map/ppermute | solution.py:14
  10.0 13.1 %copy-start.5 = (s32[1,1,8,128]{3,2,1,0:T(8,128)S(1)}, s32[1,1,8,128]{3,2,1,0:T(8,128)}, u32[]{:S(2)}) copy-start(s32[1,1,8,128]{3,2,1,0:T(8,128)} %param.16) | copy-start | bytes 12292
  10.0 21.2 %copy-start.2 = (bf16[1,1,2,5,16384]{4,2,3,1,0:T(2,128)(2,1)S(1)}, bf16[1,1,2,5,16384]{4,2,3,1,0:T(2,128)(2,1)}, u32[]{:S(2)}) copy-start(bf16[1,1,2,5,16384]{4,2,3,1,0:T(2,128)(2,1)} %param.11) | copy-start | bytes 983044
  23.1 9.4 %copy-start.6 = (s32[1,1,2,4,2,128]{5,4,3,2,1,0:T(2,128)S(1)}, s32[1,1,2,4,2,128]{5,4,3,2,1,0:T(2,128)}, u32[]{:S(2)}) copy-start(s32[1,1,2,4,2,128]{5,4,3,2,1,0:T(2,128)} %param.19) | copy-start | bytes 24580
  23.1 9.4 %copy-start.7 = (s32[2]{0:T(128)S(1)}, s32[2]{0:T(128)}, u32[]{:S(2)}) copy-start(s32[2]{0:T(128)} %constant.67) | copy-start | bytes 28
  23.1 9.5 %copy-start.8 = (s32[2]{0:T(128)S(1)}, s32[2]{0:T(128)}, u32[]{:S(2)}) copy-start(s32[2]{0:T(128)} %constant.70) | copy-start | bytes 28
  23.1 9.6 %copy-start.3 = (f32[1,1,2,16384]{3,2,1,0:T(2,128)S(1)}, f32[1,1,2,16384]{3,2,1,0:T(2,128)}, u32[]{:S(2)}) copy-start(f32[1,1,2,16384]{3,2,1,0:T(2,128)} %param.14) | copy-start | bytes 393220
  23.2 9.7 %copy-start.9 = (u32[32]{0:T(128)S(1)}, u32[32]{0:T(128)}, u32[]{:S(2)}) copy-start(u32[32]{0:T(128)} %constant.77) | copy-start | bytes 388
  23.2 10.4 %copy-start.1 = (bf16[1,1,2,25,16384]{4,2,3,1,0:T(2,128)(2,1)S(1)}, bf16[1,1,2,25,16384]{4,2,3,1,0:T(2,128)(2,1)}, u32[]{:S(2)}) copy-start(bf16[1,1,2,25,16384]{4,2,3,1,0:T(2,128)(2,1)} %param.13) | copy-start | bytes 4915204
  30.7 25.8 %collective-permute-start.2 = (bf16[1,2,20,8,128]{4,3,2,1,0:T(8,128)(2,1)S(1)}, bf16[1,2,20,8,128]{4,3,2,1,0:T(8,128)(2,1)}, u32[]{:S(2)}, u32[]{:S(2)}) collective-permute-start(bf16[1,2,20,8,128]{4,3,2,1,0:T(8,128)(2,1)S(1)} %broadcast_select_fusion), channel_id=1, source_target_pairs={{0,16},{16,0},{1,17},{17,1},{2,18},{18,2},{3,19},{19,3},{4,20},{20... | collective-permute-start | bytes 245768 | tf_op jit(solution)/shard_map/ppermute | solution.py:14
  32.2 33.5 %copy-start.4 = (f32[1,1,2,4,2,3,128]{6,4,5,3,2,1,0:T(2,128)S(1)}, f32[1,1,2,4,2,3,128]{6,4,5,3,2,1,0:T(2,128)}, u32[]{:S(2)}) copy-start(f32[1,1,2,4,2,3,128]{6,4,5,3,2,1,0:T(2,128)} %param.21) | copy-start | bytes 73732
Sparse Core Ops, SparseCore 0:
  32.4 48.3 all-gather.2
where the time goes:
time: 123 us
  other arithmetic  42 us (34%)
  local copies, waits for them, and re-layouts  35.2 us (29%)
  blocking collectives  25.1 us (20%)
  between operations  14.5 us (12%)
  matrix products  5.14 us (4%)
    unnamed x4, other arithmetic  18.8 us
    reduce_sum x7, other arithmetic, apply_jacobian(): return jnp.sum(jacobi_wide.astype(jnp.float32) * vector[:, None], axis=2)  15.2 us
    unnamed x27, local copies, waits for them, and re-layouts  13.1 us
    concatenate x1, local copies, waits for them, and re-layouts, body(): stacked = jnp.concatenate([flow, slopes], axis=1)  13.1 us
    all_gather x1, blocking collectives, body(): lax.all_gather(partner[0], 'sector', axis=0, tiled=True)  8.61 us
    unnamed x1, blocking collectives  8.42 us
    all_gather x1, blocking collectives, body(): lax.all_gather(partner[1], 'sector', axis=0, tiled=True)  8.03 us
    gather x2, local copies, waits for them, and re-layouts, body(): jnp.take(stacked, face_cells.reshape(-1), axis=2)  7.46 us
  transfers between devices with their start and end apart: 4, of which 0 were waited for; matrix products, arithmetic and copies ran while one was open for 51% of the time, Pallas kernels for 0%

commit v1 on v0

v1 whole, which is shorter than its diff:
```python
import functools
import math

import jax
import jax.numpy as jnp
import numpy as np
from jax import lax
from jax.experimental import pallas as pl
from jax.experimental.pallas import tpu as pltpu
from jax.sharding import PartitionSpec as P

SWEEPS = 6
LANES = 128
WIDE = 256
SLOT_ROWS = 32
STAGE_ROWS = 48
MESH = pl.DeviceIdType.MESH
VMEM_LIMIT = 48 * 1024 * 1024


def spectral_matrix(period):
    index = np.arange(period)
    gap = index[:, None] - index[None, :]
    safe_gap = np.where(gap == 0, 1, gap)
    angle = safe_gap * (math.pi / period)
    entry = 0.5 * (1 - 2 * (np.abs(gap) % 2)) * np.cos(angle) / np.sin(angle)
    return np.where(gap == 0, 0.0, entry).astype(np.float32)


def one_hot_rows(index_row):
    rows = lax.broadcasted_iota(jnp.int32, (WIDE, index_row.shape[1]), 0)
    return jnp.where(rows == index_row, 1.0, 0.0).astype(jnp.bfloat16)


def gather_kernel(capacity, count_ref, matching_ref, donor_ref, state_ref, grad_ref, send_ref, source):
    inst_local, nvar, cells = state_ref.shape
    nslope = grad_ref.shape[1]
    slots = donor_ref.shape[0]
    sectors = send_ref.shape[0]
    columns = sectors * capacity * LANES
    part = min(columns, 1024)
    source[...] = jnp.zeros_like(source)
    for t in range(inst_local):
        source[t, 0:nvar, :] = state_ref[t]
        source[t, 16 : 16 + nslope, :] = grad_ref[t]
    block_id = lax.broadcasted_iota(jnp.int32, (1, columns), 1) // LANES
    block_sector = block_id // capacity
    block_rank = block_id % capacity
    group = 4
    for t in range(inst_local):
        index_row = jnp.full((1, columns), -1, jnp.int32)
        seen = jnp.zeros((1, columns), jnp.int32)
        for b in range(slots):
            target = jnp.where(b < count_ref[0], matching_ref[t, b], -1)
            hit = block_sector == target
            cells_row = jnp.concatenate([donor_ref[b : b + 1, :]] * (columns // LANES), axis=1)
            index_row = jnp.where(hit & (seen == block_rank), cells_row, index_row)
            seen = seen + jnp.where(hit, 1, 0)
        for first in range(0, columns, part):
            piece = index_row[:, first : first + part]
            high = piece >> 8
            hot = one_hot_rows(piece & (WIDE - 1))

            def step(g, total):
                rows = [
                    source[t, :, pl.ds(pl.multiple_of((g * group + j) * WIDE, WIDE), WIDE)]
                    for j in range(group)
                ]
                picked = jnp.dot(
                    jnp.concatenate(rows, axis=0), hot, preferred_element_type=jnp.float32
                )
                for j in range(group):
                    mine = picked[j * SLOT_ROWS : (j + 1) * SLOT_ROWS]
                    total = total + jnp.where(high == g * group + j, mine, 0.0)
                return total

            total = lax.fori_loop(
                0, cells // WIDE // group, step, jnp.zeros((SLOT_ROWS, part), jnp.float32)
            ).astype(jnp.bfloat16)
            for j in range(part // LANES):
                d, k = divmod(first // LANES + j, capacity)
                send_ref[d, (t * capacity + k) * SLOT_ROWS : (t * capacity + k + 1) * SLOT_ROWS, :] = (
                    total[:, j * LANES : (j + 1) * LANES]
                )


def exchange_kernel(sectors, insts, send_ref, state_ref, recv_ref, all_ref, fs, fr, ss, sr, own):
    row = lax.axis_index("row")
    sector = lax.axis_index("sector")
    inst = lax.axis_index("inst")
    barrier = pltpu.get_barrier_semaphore()
    for d in range(sectors):
        pl.semaphore_signal(barrier, inc=1, device_id=(1 - row, d, inst), device_id_type=MESH)
    for step in range(1, insts):
        pl.semaphore_signal(
            barrier, inc=1, device_id=(row, sector, (inst + step) % insts), device_id_type=MESH
        )
    pl.semaphore_wait(barrier, sectors + insts - 1)
    copies = []
    for step in range(1, insts):
        peer = (inst + step) % insts
        copies.append(
            pltpu.make_async_remote_copy(
                src_ref=state_ref,
                dst_ref=all_ref.at[inst],
                send_sem=ss.at[step - 1],
                recv_sem=sr.at[step - 1],
                device_id=(row, sector, peer),
                device_id_type=MESH,
            )
        )
    for step in range(sectors):
        peer = (sector + step) % sectors
        copies.append(
            pltpu.make_async_remote_copy(
                src_ref=send_ref.at[peer],
                dst_ref=recv_ref.at[sector],
                send_sem=fs.at[step],
                recv_sem=fr.at[step],
                device_id=(1 - row, peer, inst),
                device_id_type=MESH,
            )
        )
    for copy in copies:
        copy.start()
    mine = pltpu.make_async_copy(state_ref, all_ref.at[inst], own)
    mine.start()
    mine.wait()
    for copy in copies:
        copy.wait()


def update_kernel(
    dmat_ref, freq_ref, recv_ref, weights_ref, offsets_ref, targets_ref, all_ref, state_ref,
    jac_ref, pseudo_ref, out_ref, faces, coupling, stage, out_stage,
):
    inst_local, nvar, cells = state_ref.shape
    sectors, capacity = targets_ref.shape[1:3]
    insts = all_ref.shape[0]
    first_row = lax.axis_index("inst") * inst_local
    rotation = freq_ref[0]
    faces[...] = jnp.zeros_like(faces)
    group = 4
    for t in range(inst_local):
        target_rows = []
        for m in range(sectors):
            for k in range(capacity):
                slot = t * capacity + k
                column = (m * capacity + k) * LANES
                mixed = jnp.dot(
                    recv_ref[m, slot * SLOT_ROWS : (slot + 1) * SLOT_ROWS, :],
                    weights_ref[t, m, k],
                    preferred_element_type=jnp.float32,
                )
                value = mixed[0:nvar]
                for d in range(3):
                    begin = 16 + d * nvar
                    value = value + offsets_ref[t, m, k, d : d + 1, :] * mixed[begin : begin + nvar]
                upper = value.astype(jnp.bfloat16).astype(jnp.float32)
                faces[t, 0:nvar, column : column + LANES] = upper
                faces[t, 8 : 8 + nvar, column : column + LANES] = value - upper
                target_rows.append(targets_ref[t, m, k : k + 1, :])
        target_row = jnp.concatenate(target_rows, axis=1)
        high = target_row >> 8
        hot = one_hot_rows(target_row & (WIDE - 1))

        def spread(g, carry):
            face_values = faces[t]
            rows = [jnp.where(high == g * group + j, face_values, 0.0) for j in range(group)]
            placed = lax.dot_general(
                jnp.concatenate(rows, axis=0).astype(jnp.bfloat16),
                hot,
                (((1,), (1,)), ((), ())),
                preferred_element_type=jnp.float32,
            )
            for j in range(group):
                begin = pl.multiple_of((g * group + j) * WIDE, WIDE)
                coupling[t, :, pl.ds(begin, WIDE)] = (
                    placed[j * 16 : j * 16 + 8] + placed[j * 16 + 8 : j * 16 + 16]
                )
            return carry

        lax.fori_loop(0, cells // WIDE // group, spread, 0)

    chunk = 8 * LANES
    for t in range(inst_local):
        coefs = [
            [dmat_ref[first_row + t, i * inst_local + u] * rotation for u in range(inst_local)]
            for i in range(insts)
        ]

        def relax(c, carry):
            window = pl.ds(pl.multiple_of(c * chunk, chunk), chunk)
            jac = jac_ref[t, :, window].astype(jnp.float32)
            flow = state_ref[t, :, window].astype(jnp.float32)
            pseudo = pseudo_ref[t : t + 1, window]
            rest = -coupling[t, 0:nvar, window]
            for i in range(insts):
                for u in range(inst_local):
                    rest = rest + coefs[i][u] * all_ref[i, u, :, window].astype(jnp.float32)
            for j in range(8):
                lanes = slice(j * LANES, (j + 1) * LANES)
                at = j * STAGE_ROWS
                stage[at : at + nvar * nvar, :] = jac[:, lanes]
                stage[at + 32 : at + 32 + nvar, :] = rest[:, lanes]
                stage[at + 40 : at + 40 + nvar, :] = flow[:, lanes]
                stage[at + 46 : at + 47, :] = pseudo[:, lanes]

            def row(r):
                return stage[pl.ds(r, 8, stride=STAGE_ROWS), :]

            matrix = [[row(v * nvar + w) for w in range(nvar)] for v in range(nvar)]
            base = [row(40 + v) for v in range(nvar)]
            shift = -row(46)

            def apply(start, vector):
                result = []
                for v in range(nvar):
                    acc = start[v]
                    for w in range(nvar):
                        acc = acc + matrix[v][w] * vector[w]
                    result.append(acc)
                return result

            residual = apply([row(32 + v) for v in range(nvar)], base)
            increment = [shift * value for value in residual]
            for sweep in range(SWEEPS):
                increment = [shift * value for value in apply(residual, increment)]
            for v in range(nvar):
                out_stage[pl.ds(v, 8, stride=8), :] = base[v] + increment[v]
            for j in range(8):
                begin = pl.multiple_of(c * chunk + j * LANES, LANES)
                out_ref[t, :, pl.ds(begin, LANES)] = out_stage[j * 8 : j * 8 + nvar, :]
            return carry

        lax.fori_loop(0, cells // chunk, relax, 0)


def body(
    state,
    gradients,
    jacobian,
    pseudo_step,
    frequency,
    donor_cells,
    block_count,
    matching,
    target_cells,
    interp_weights,
    face_offsets,
):
    flow = state[0, 0]
    inst_local, nvar, cells = flow.shape
    sectors = lax.axis_size("sector")
    insts = lax.axis_size("inst")
    capacity = target_cells.shape[4]
    columns = sectors * capacity * LANES
    vmem = pl.BlockSpec(memory_space=pltpu.VMEM)
    smem = pl.BlockSpec(memory_space=pltpu.SMEM)
    hbm = pl.BlockSpec(memory_space=pl.ANY)
    packet = jax.ShapeDtypeStruct((sectors, inst_local * capacity * SLOT_ROWS, LANES), jnp.bfloat16)
    send = pl.pallas_call(
        functools.partial(gather_kernel, capacity),
        out_shape=packet,
        in_specs=[smem, smem, vmem, vmem, vmem],
        out_specs=vmem,
        scratch_shapes=[pltpu.VMEM((inst_local, SLOT_ROWS, cells), jnp.bfloat16)],
        compiler_params=pltpu.CompilerParams(vmem_limit_bytes=VMEM_LIMIT),
    )(block_count.reshape(1), matching[0, 0], donor_cells[0, 0], flow, gradients[0, 0])
    recv, everything = pl.pallas_call(
        functools.partial(exchange_kernel, sectors, insts),
        out_shape=(packet, jax.ShapeDtypeStruct((insts,) + flow.shape, flow.dtype)),
        in_specs=[hbm, hbm],
        out_specs=(hbm, hbm),
        scratch_shapes=[
            pltpu.SemaphoreType.DMA((sectors,)),
            pltpu.SemaphoreType.DMA((sectors,)),
            pltpu.SemaphoreType.DMA((insts - 1,)),
            pltpu.SemaphoreType.DMA((insts - 1,)),
            pltpu.SemaphoreType.DMA,
        ],
        compiler_params=pltpu.CompilerParams(collective_id=0, has_side_effects=True),
    )(send, flow)
    dmat = jnp.asarray(spectral_matrix(inst_local * insts))
    result = pl.pallas_call(
        update_kernel,
        out_shape=jax.ShapeDtypeStruct(flow.shape, jnp.float32),
        in_specs=[smem, smem] + [vmem] * 8,
        out_specs=vmem,
        scratch_shapes=[
            pltpu.VMEM((inst_local, 16, columns), jnp.float32),
            pltpu.VMEM((inst_local, 8, cells), jnp.float32),
            pltpu.VMEM((8 * STAGE_ROWS, LANES), jnp.float32),
            pltpu.VMEM((64, LANES), jnp.float32),
        ],
        compiler_params=pltpu.CompilerParams(vmem_limit_bytes=VMEM_LIMIT),
    )(
        dmat,
        frequency,
        recv,
        interp_weights[0, 0],
        face_offsets[0, 0],
        target_cells[0, 0],
        everything,
        flow,
        jacobian[0, 0],
        pseudo_step[0, 0],
    )
    return result[None, None]


def solution(mesh):
    placed = (
        P("row", "sector", "inst", None, None),
        P("row", "sector", "inst", None, None),
        P("row", "sector", "inst", None, None),
        P("row", "sector", "inst", None),
        P("row"),
        P("row", "sector", None, None),
        P("row", "sector"),
        P("row", "sector", "inst", None),
        P("row", "sector", "inst", None, None, None),
        P("row", "sector", "inst", None, None, None, None),
        P("row", "sector", "inst", None, None, None, None),
    )
    return jax.shard_map(
        body,
        mesh=mesh,
        in_specs=placed,
        out_specs=P("row", "sector", "inst", None, None),
        check_vma=False,
    )
```

time: 123 us -> 89 us (0.72)
  the two profiles are of different devices: /device:TPU:0 before, /device:TPU:9 now
where the time goes in v1:
time: 89 us; the launch traced here: 88.6 us
  Pallas kernels  75.4 us (85%)
  local copies, waits for them, and re-layouts  11.8 us (13%)
  between operations  1.45 us (2%)
    pallas_call x1, Pallas kernels, body(): pl.pallas_call(functools.partial(exchange_kernel, sectors, insts), out_sh...  50.7 us
    pallas_call x1, Pallas kernels, body(): pl.pallas_call(update_kernel, out_shape=jax.ShapeDtypeStruct(flow.shape,...  15.7 us
    unnamed x28, local copies, waits for them, and re-layouts  10.4 us
    pallas_call x1, Pallas kernels, body(): pl.pallas_call(functools.partial(gather_kernel, capacity), out_shape=pack...  8.92 us

profile of v1, /device:TPU:9, one launch (start us, length us, event | category | flops | bytes accessed | tf_op | source)
XLA Modules:
  0.0 88.6 jit_solution(17766671430392390556)
XLA Ops:
  0.0 0.0 copy-start.10
  0.0 0.0 copy-start.8
  1.3 0.8 copy.25
  2.1 0.0 copy-start.11
  2.1 1.3 %copy.24 = bf16[1,1,2,5,16384]{4,3,2,1,0:T(8,128)(2,1)S(1)} copy(bf16[1,1,2,5,16384]{4,2,3,1,0:T(2,128)(2,1)} %param.12) | data formatting | bytes 655360 | tf_op args[0]
  3.4 0.0 copy-start
  3.4 1.9 %copy.23 = bf16[1,1,2,15,16384]{4,3,2,1,0:T(8,128)(2,1)S(1)} copy(bf16[1,1,2,15,16384]{4,2,3,1,0:T(2,128)(2,1)} %param.13) | data formatting | bytes 1966080 | tf_op args[1]
  5.3 0.0 copy-done.10
  5.3 0.0 copy-done.8
  5.4 8.9 %shard_map.118.send_ref = bf16[4,128,128]{2,1,0:T(8,128)(2,1)S(1)} custom-call(s32[1]{0:T(128)} %bitcast.19.count_ref, s32[2,8]{1,0:T(2,128)S(1)} %bitcast.30, s32[8,128]{1,0:T(8,128)S(1)} %bitcast.29, bf16[2,5,16384]{2,1,0:T(8,128)(2,1)S(1)} %bitcast.20, bf16[2,15,16384]{2,1,0:T(8,128)(2,1)S(1)} %bitcast.23), custom_call_target="tpu_custom_call" | custom-call | tf_op jit(solution)/shard_map/pallas_call | solution.py:262
  14.3 0.0 copy-start.4
  14.3 0.6 copy-done.4
  14.9 0.0 copy-done.11
  14.9 0.0 copy-start.3
  14.9 0.0 copy-start.5
  14.9 0.0 copy-start.7
  14.9 0.0 copy-start.9
  15.0 2.2 %copy.22 = bf16[1,1,2,25,16384]{4,3,2,1,0:T(8,128)(2,1)} copy(bf16[1,1,2,25,16384]{4,2,3,1,0:T(2,128)(2,1)S(1)} %copy-done.11) | data formatting | bytes 3276800 | tf_op args[2]
  17.2 0.0 copy-done
  17.2 50.7 %shard_map.119 = (bf16[4,128,128]{2,1,0:T(8,128)(2,1)}, bf16[4,2,5,16384]{3,2,1,0:T(8,128)(2,1)}) custom-call(bf16[4,128,128]{2,1,0:T(8,128)(2,1)} %copy-done.4, bf16[2,5,16384]{2,1,0:T(8,128)(2,1)} %bitcast.21), custom_call_target="tpu_custom_call" | custom-call | tf_op jit(solution)/shard_map/pallas_call | solution.py:270
  68.0 0.0 copy-done.3
  68.0 0.0 copy-done.5
  68.0 0.0 copy-done.7
  68.0 0.0 copy-done.9
  68.0 0.0 copy-start.1
  68.0 1.0 %copy-done.1 = bf16[1,1,2,5,16384]{4,3,2,1,0:T(8,128)(2,1)S(1)} copy-done((bf16[1,1,2,5,16384]{4,3,2,1,0:T(8,128)(2,1)S(1)}, bf16[1,1,2,5,16384]{4,3,2,1,0:T(8,128)(2,1)}, u32[]{:S(2)}) %copy-start.1) | copy-done | bytes 327704
  69.0 0.0 copy-start.2
  69.0 1.6 %copy-done.2 = bf16[4,2,5,16384]{3,2,1,0:T(8,128)(2,1)S(1)} copy-done((bf16[4,2,5,16384]{3,2,1,0:T(8,128)(2,1)S(1)}, bf16[4,2,5,16384]{3,2,1,0:T(8,128)(2,1)}, u32[]{:S(2)}) %copy-start.2) | copy-done | bytes 1310744
  70.6 0.0 copy-start.6
  70.6 0.9 %copy-done.6 = bf16[4,128,128]{2,1,0:T(8,128)(2,1)S(1)} copy-done((bf16[4,128,128]{2,1,0:T(8,128)(2,1)S(1)}, bf16[4,128,128]{2,1,0:T(8,128)(2,1)}, u32[]{:S(2)}) %copy-start.6) | copy-done | bytes 131096
  71.5 15.7 %shard_map.120 = f32[2,5,16384]{2,1,0:T(8,128)S(1)} custom-call(f32[8,8]{1,0:T(8,128)S(1)} %copy-done.9, f32[1]{0:T(128)S(6)} %copy.26.freq_ref, bf16[4,128,128]{2,1,0:T(8,128)(2,1)S(1)} %copy-done.6, bf16[2,4,2,128,128]{4,3,2,1,0:T(8,128)(2,1)S(1)} %bitcast.25, f32[2,4,2,3,128]{4,3,2,1,0:T(4,128)S(1)} %bitcast.26, s32[2,4,2,128]{3,2,1,0:T(2,128)S(1)} %bitcast.28, ...), custom_call_target="tpu_custom_call" | custom-call | tf_op jit(solution)/shard_map/pallas_call | solution.py:285
  87.3 1.3 %copy.17 = f32[1,1,2,5,16384]{4,2,3,1,0:T(2,128)} copy(f32[1,1,2,5,16384]{4,3,2,1,0:T(8,128)S(1)} %bitcast.24) | data formatting | bytes 1310720 | tf_op jit(solution)/shard_map/broadcast_in_dim | solution.py:309
Async XLA Ops:
  0.0 5.3 %copy-start.10 = (s32[1,1,2,8]{3,2,1,0:T(2,128)S(1)}, s32[1,1,2,8]{3,2,1,0:T(2,128)}, u32[]{:S(2)}) copy-start(s32[1,1,2,8]{3,2,1,0:T(2,128)} %param.19) | copy-start | bytes 196
  0.0 5.3 %copy-start.8 = (s32[1,1,8,128]{3,2,1,0:T(8,128)S(1)}, s32[1,1,8,128]{3,2,1,0:T(8,128)}, u32[]{:S(2)}) copy-start(s32[1,1,8,128]{3,2,1,0:T(8,128)} %param.17) | copy-start | bytes 12292
  2.1 12.9 %copy-start.11 = (bf16[1,1,2,25,16384]{4,2,3,1,0:T(2,128)(2,1)S(1)}, bf16[1,1,2,25,16384]{4,2,3,1,0:T(2,128)(2,1)}, u32[]{:S(2)}) copy-start(bf16[1,1,2,25,16384]{4,2,3,1,0:T(2,128)(2,1)} %param.14) | copy-start | bytes 4915204
  3.4 13.8 %copy-start = (bf16[1,1,2,5,16384]{4,3,2,1,0:T(8,128)(2,1)}, bf16[1,1,2,5,16384]{4,3,2,1,0:T(8,128)(2,1)S(1)}, u32[]{:S(2)}) copy-start(bf16[1,1,2,5,16384]{4,3,2,1,0:T(8,128)(2,1)S(1)} %copy.24) | copy-start | bytes 983044
  14.3 0.7 copy-start.4
  14.9 53.0 %copy-start.3 = (bf16[1,1,2,4,2,128,128]{6,5,4,3,2,1,0:T(8,128)(2,1)S(1)}, bf16[1,1,2,4,2,128,128]{6,5,4,3,2,1,0:T(8,128)(2,1)}, u32[]{:S(2)}) copy-start(bf16[1,1,2,4,2,128,128]{6,5,4,3,2,1,0:T(8,128)(2,1)} %param.21) | copy-start | bytes 1572868
  14.9 53.0 %copy-start.5 = (f32[1,1,2,16384]{3,2,1,0:T(2,128)S(1)}, f32[1,1,2,16384]{3,2,1,0:T(2,128)}, u32[]{:S(2)}) copy-start(f32[1,1,2,16384]{3,2,1,0:T(2,128)} %param.15) | copy-start | bytes 393220
  14.9 53.0 %copy-start.7 = (s32[1,1,2,4,2,128]{5,4,3,2,1,0:T(2,128)S(1)}, s32[1,1,2,4,2,128]{5,4,3,2,1,0:T(2,128)}, u32[]{:S(2)}) copy-start(s32[1,1,2,4,2,128]{5,4,3,2,1,0:T(2,128)} %param.20) | copy-start | bytes 24580
  14.9 53.0 %copy-start.9 = (f32[8,8]{1,0:T(8,128)S(1)}, f32[8,8]{1,0:T(8,128)}, u32[]{:S(2)}) copy-start(f32[8,8]{1,0:T(8,128)} %constant.2.clone.dmat_ref) | copy-start | bytes 772
  68.0 1.0 %copy-start.1 = (bf16[1,1,2,5,16384]{4,3,2,1,0:T(8,128)(2,1)S(1)}, bf16[1,1,2,5,16384]{4,3,2,1,0:T(8,128)(2,1)}, u32[]{:S(2)}) copy-start(bf16[1,1,2,5,16384]{4,3,2,1,0:T(8,128)(2,1)} %copy-done) | copy-start | bytes 983044
  69.0 1.6 %copy-start.2 = (bf16[4,2,5,16384]{3,2,1,0:T(8,128)(2,1)S(1)}, bf16[4,2,5,16384]{3,2,1,0:T(8,128)(2,1)}, u32[]{:S(2)}) copy-start(bf16[4,2,5,16384]{3,2,1,0:T(8,128)(2,1)} %get-tuple-element.8.all_ref) | copy-start | bytes 3932164
  70.6 0.9 %copy-start.6 = (bf16[4,128,128]{2,1,0:T(8,128)(2,1)S(1)}, bf16[4,128,128]{2,1,0:T(8,128)(2,1)}, u32[]{:S(2)}) copy-start(bf16[4,128,128]{2,1,0:T(8,128)(2,1)} %get-tuple-element.7.recv_ref) | copy-start | bytes 393220

commit v2 on v1

--- a/solution.py
+++ b/solution.py
@@ -194,10 +194,14 @@
             jac = jac_ref[t, :, window].astype(jnp.float32)
             flow = state_ref[t, :, window].astype(jnp.float32)
             pseudo = pseudo_ref[t : t + 1, window]
-            rest = -coupling[t, 0:nvar, window]
+            position = lax.broadcasted_iota(jnp.int32, (inst_local, chunk), 0)
+            mixture = jnp.zeros((nvar, inst_local, chunk), jnp.float32)
             for i in range(insts):
+                factor = jnp.zeros((inst_local, chunk), jnp.float32)
                 for u in range(inst_local):
-                    rest = rest + coefs[i][u] * all_ref[i, u, :, window].astype(jnp.float32)
+                    factor = jnp.where(position == u, coefs[i][u], factor)
+                mixture = mixture + factor[None] * all_ref[i, :, :, window].astype(jnp.float32)
+            rest = jnp.sum(mixture, axis=1) - coupling[t, 0:nvar, window]
             for j in range(8):
                 lanes = slice(j * LANES, (j + 1) * LANES)
                 at = j * STAGE_ROWS
@@ -267,9 +271,10 @@
         scratch_shapes=[pltpu.VMEM((inst_local, SLOT_ROWS, cells), jnp.bfloat16)],
         compiler_params=pltpu.CompilerParams(vmem_limit_bytes=VMEM_LIMIT),
     )(block_count.reshape(1), matching[0, 0], donor_cells[0, 0], flow, gradients[0, 0])
+    compact = flow.transpose(1, 0, 2)
     recv, everything = pl.pallas_call(
         functools.partial(exchange_kernel, sectors, insts),
-        out_shape=(packet, jax.ShapeDtypeStruct((insts,) + flow.shape, flow.dtype)),
+        out_shape=(packet, jax.ShapeDtypeStruct((insts,) + compact.shape, flow.dtype)),
         in_specs=[hbm, hbm],
         out_specs=(hbm, hbm),
         scratch_shapes=[
@@ -280,7 +285,7 @@
             pltpu.SemaphoreType.DMA,
         ],
         compiler_params=pltpu.CompilerParams(collective_id=0, has_side_effects=True),
-    )(send, flow)
+    )(send, compact)
     dmat = jnp.asarray(spectral_matrix(inst_local * insts))
     result = pl.pallas_call(
         update_kernel,

time: 89 us -> 69.4 us (0.78)
  Pallas kernels: 75.4 us -> 60.6 us
  local copies, waits for them, and re-layouts: 11.8 us -> 7 us
    pallas_call x1, Pallas kernels: 50.7 us -> 33.9 us  [body(): pl.pallas_call(functools.partial(exchange_kernel, sectors, insts), out_sh...]
    unnamed x28 -> x26, local copies, waits for them, and re-layouts: 10.4 us -> 4.56 us
    pallas_call x1, Pallas kernels: 15.7 us -> 17.8 us  [body(): pl.pallas_call(update_kernel, out_shape=jax.ShapeDtypeStruct(flow.shape,...]
    transpose x0 -> x1, local copies, waits for them, and re-layouts: none -> 1.1 us  [body(): compact = flow.transpose(1, 0, 2)]
where the time goes in v2:
time: 69.4 us; the launch traced here: 69.1 us
  Pallas kernels  60.6 us (87%)
  local copies, waits for them, and re-layouts  7 us (10%)
  between operations  1.51 us (2%)
    pallas_call x1, Pallas kernels, body(): pl.pallas_call(functools.partial(exchange_kernel, sectors, insts), out_sh...  33.9 us
    pallas_call x1, Pallas kernels, body(): pl.pallas_call(update_kernel, out_shape=jax.ShapeDtypeStruct(flow.shape,...  17.8 us
    pallas_call x1, Pallas kernels, body(): pl.pallas_call(functools.partial(gather_kernel, capacity), out_shape=pack...  8.92 us
    unnamed x26, local copies, waits for them, and re-layouts  4.56 us

profile of v2, /device:TPU:9, one launch (start us, length us, event | category | flops | bytes accessed | tf_op | source)
XLA Modules:
  0.0 69.1 jit_solution(8673219389540258105)
XLA Ops:
  0.0 0.0 copy-start.10
  1.4 0.8 %copy.27 = f32[1,1,2,4,2,3,128]{6,5,4,3,2,1,0:T(4,128)S(1)} copy(f32[1,1,2,4,2,3,128]{6,4,5,3,2,1,0:T(2,128)} %param.22) | data formatting | bytes 49152 | tf_op args[10]
  2.1 1.2 %copy.26 = bf16[1,1,2,5,16384]{4,3,2,1,0:T(8,128)(2,1)S(1)} copy(bf16[1,1,2,5,16384]{4,2,3,1,0:T(2,128)(2,1)} %param.12) | data formatting | bytes 655360 | tf_op args[0]
  3.3 0.0 copy-start.6
  3.3 0.0 copy-start.8
  3.3 1.1 %copy.15.state_ref = bf16[5,2,16384]{2,1,0:T(2,128)(2,1)} copy(bf16[5,2,16384]{2,0,1:T(8,128)(2,1)S(1)} %bitcast.24) | data formatting | bytes 655360 | tf_op jit(solution)/shard_map/transpose | solution.py:274
  4.4 0.0 copy-done.10
  4.4 0.0 copy-start.9
  4.4 0.5 copy.25
  5.0 0.0 copy-done.6
  5.0 0.0 copy-done.8
  5.0 8.9 %shard_map.118.send_ref = bf16[4,128,128]{2,1,0:T(8,128)(2,1)S(1)} custom-call(s32[1]{0:T(128)} %bitcast.22.count_ref, s32[2,8]{1,0:T(2,128)S(1)} %bitcast.34, s32[8,128]{1,0:T(8,128)S(1)} %bitcast.33, bf16[2,5,16384]{2,1,0:T(8,128)(2,1)S(1)} %bitcast.25, bf16[2,15,16384]{2,1,0:T(8,128)(2,1)S(1)} %bitcast.27), custom_call_target="tpu_custom_call" | custom-call | tf_op jit(solution)/shard_map/pallas_call | solution.py:266
  13.9 0.0 copy-start.1
  13.9 0.6 copy-done.1
  14.6 33.9 %shard_map.119 = (bf16[4,128,128]{2,1,0:T(8,128)(2,1)}, bf16[4,5,2,16384]{3,2,1,0:T(2,128)(2,1)}) custom-call(bf16[4,128,128]{2,1,0:T(8,128)(2,1)} %copy-done.1, bf16[5,2,16384]{2,1,0:T(2,128)(2,1)} %copy.15.state_ref), custom_call_target="tpu_custom_call" | custom-call | tf_op jit(solution)/shard_map/pallas_call | solution.py:275
  48.5 0.0 copy-done.9
  48.5 0.0 copy-start
  48.5 0.0 copy-start.2
  48.5 0.0 copy-start.3
  48.5 0.0 copy-start.4
  48.5 0.0 copy-start.5
  48.5 0.0 copy-start.7
  48.5 0.9 %copy.24 = bf16[1,1,2,25,16384]{4,3,2,1,0:T(8,128)(2,1)S(1)} copy(bf16[1,1,2,25,16384]{4,2,3,1,0:T(2,128)(2,1)S(1)} %copy-done.9) | data formatting | bytes 3276800 | tf_op args[2]
  49.5 0.3 copy-done
  49.8 0.1 copy-done.2
  49.9 0.0 copy-done.3
  49.9 0.0 copy-done.4
  50.0 0.0 copy-done.5
  50.0 0.0 copy-done.7
  50.0 17.8 %shard_map.120 = f32[2,5,16384]{2,1,0:T(8,128)S(1)} custom-call(f32[8,8]{1,0:T(8,128)S(1)} %copy-done.7, f32[1]{0:T(128)S(6)} %copy.28.freq_ref, bf16[4,128,128]{2,1,0:T(8,128)(2,1)S(1)} %copy-done.4, bf16[2,4,2,128,128]{4,3,2,1,0:T(8,128)(2,1)S(1)} %bitcast.29, f32[2,4,2,3,128]{4,3,2,1,0:T(4,128)S(1)} %bitcast.30, s32[2,4,2,128]{3,2,1,0:T(2,128)S(1)} %bitcast.32, ...), custom_call_target="tpu_custom_call" | custom-call | tf_op jit(solution)/shard_map/pallas_call | solution.py:290
  67.8 1.3 %copy.18 = f32[1,1,2,5,16384]{4,2,3,1,0:T(2,128)} copy(f32[1,1,2,5,16384]{4,3,2,1,0:T(8,128)S(1)} %bitcast.28) | data formatting | bytes 1310720 | tf_op jit(solution)/shard_map/broadcast_in_dim | solution.py:314
Async XLA Ops:
  0.0 4.4 %copy-start.10 = (bf16[1,1,2,15,16384]{4,2,3,1,0:T(2,128)(2,1)S(1)}, bf16[1,1,2,15,16384]{4,2,3,1,0:T(2,128)(2,1)}, u32[]{:S(2)}) copy-start(bf16[1,1,2,15,16384]{4,2,3,1,0:T(2,128)(2,1)} %param.13) | copy-start | bytes 2949124
  3.3 1.7 %copy-start.6 = (s32[1,1,8,128]{3,2,1,0:T(8,128)S(1)}, s32[1,1,8,128]{3,2,1,0:T(8,128)}, u32[]{:S(2)}) copy-start(s32[1,1,8,128]{3,2,1,0:T(8,128)} %param.17) | copy-start | bytes 12292
  3.3 1.7 %copy-start.8 = (s32[1,1,2,8]{3,2,1,0:T(2,128)S(1)}, s32[1,1,2,8]{3,2,1,0:T(2,128)}, u32[]{:S(2)}) copy-start(s32[1,1,2,8]{3,2,1,0:T(2,128)} %param.19) | copy-start | bytes 196
  4.4 44.0 %copy-start.9 = (bf16[1,1,2,25,16384]{4,2,3,1,0:T(2,128)(2,1)S(1)}, bf16[1,1,2,25,16384]{4,2,3,1,0:T(2,128)(2,1)}, u32[]{:S(2)}) copy-start(bf16[1,1,2,25,16384]{4,2,3,1,0:T(2,128)(2,1)} %param.14) | copy-start | bytes 4915204
  13.9 0.6 copy-start.1
  48.5 1.3 %copy-start = (bf16[4,5,2,16384]{3,2,1,0:T(2,128)(2,1)S(1)}, bf16[4,5,2,16384]{3,2,1,0:T(2,128)(2,1)}, u32[]{:S(2)}) copy-start(bf16[4,5,2,16384]{3,2,1,0:T(2,128)(2,1)} %get-tuple-element.8.all_ref) | copy-start | bytes 3932164
  48.5 1.4 %copy-start.2 = (bf16[1,1,2,4,2,128,128]{6,5,4,3,2,1,0:T(8,128)(2,1)S(1)}, bf16[1,1,2,4,2,128,128]{6,5,4,3,2,1,0:T(8,128)(2,1)}, u32[]{:S(2)}) copy-start(bf16[1,1,2,4,2,128,128]{6,5,4,3,2,1,0:T(8,128)(2,1)} %param.21) | copy-start | bytes 1572868
  48.5 1.4 %copy-start.3 = (f32[1,1,2,16384]{3,2,1,0:T(2,128)S(1)}, f32[1,1,2,16384]{3,2,1,0:T(2,128)}, u32[]{:S(2)}) copy-start(f32[1,1,2,16384]{3,2,1,0:T(2,128)} %param.15) | copy-start | bytes 393220
  48.5 1.5 %copy-start.4 = (bf16[4,128,128]{2,1,0:T(8,128)(2,1)S(1)}, bf16[4,128,128]{2,1,0:T(8,128)(2,1)}, u32[]{:S(2)}) copy-start(bf16[4,128,128]{2,1,0:T(8,128)(2,1)} %get-tuple-element.7.recv_ref) | copy-start | bytes 393220
  48.5 1.5 %copy-start.5 = (s32[1,1,2,4,2,128]{5,4,3,2,1,0:T(2,128)S(1)}, s32[1,1,2,4,2,128]{5,4,3,2,1,0:T(2,128)}, u32[]{:S(2)}) copy-start(s32[1,1,2,4,2,128]{5,4,3,2,1,0:T(2,128)} %param.20) | copy-start | bytes 24580
  48.5 1.4 %copy-start.7 = (f32[8,8]{1,0:T(8,128)S(1)}, f32[8,8]{1,0:T(8,128)}, u32[]{:S(2)}) copy-start(f32[8,8]{1,0:T(8,128)} %constant.2.clone.dmat_ref) | copy-start | bytes 772

commit v3 on v2

--- a/solution.py
+++ b/solution.py
@@ -32,7 +32,7 @@
     return jnp.where(rows == index_row, 1.0, 0.0).astype(jnp.bfloat16)
 
 
-def gather_kernel(capacity, count_ref, matching_ref, donor_ref, state_ref, grad_ref, send_ref, source):
+def gather_faces(capacity, count_ref, matching_ref, donor_ref, state_ref, grad_ref, send_ref, source):
     inst_local, nvar, cells = state_ref.shape
     nslope = grad_ref.shape[1]
     slots = donor_ref.shape[0]
@@ -84,7 +84,10 @@
                 )
 
 
-def exchange_kernel(sectors, insts, send_ref, state_ref, recv_ref, all_ref, fs, fr, ss, sr, own):
+def exchange_kernel(
+    sectors, insts, capacity, count_ref, matching_ref, donor_ref, flow_ref, grad_ref, state_ref,
+    recv_ref, all_ref, source, send_ref, fs, fr, ss, sr, own,
+):
     row = lax.axis_index("row")
     sector = lax.axis_index("sector")
     inst = lax.axis_index("inst")
@@ -109,22 +112,25 @@
                 device_id_type=MESH,
             )
         )
-    for step in range(sectors):
-        peer = (sector + step) % sectors
-        copies.append(
-            pltpu.make_async_remote_copy(
-                src_ref=send_ref.at[peer],
-                dst_ref=recv_ref.at[sector],
-                send_sem=fs.at[step],
-                recv_sem=fr.at[step],
-                device_id=(1 - row, peer, inst),
-                device_id_type=MESH,
-            )
-        )
     for copy in copies:
         copy.start()
     mine = pltpu.make_async_copy(state_ref, all_ref.at[inst], own)
     mine.start()
+    gather_faces(
+        capacity, count_ref, matching_ref, donor_ref, flow_ref, grad_ref, send_ref, source
+    )
+    for step in range(sectors):
+        peer = (sector + step) % sectors
+        copy = pltpu.make_async_remote_copy(
+            src_ref=send_ref.at[peer],
+            dst_ref=recv_ref.at[sector],
+            send_sem=fs.at[step],
+            recv_sem=fr.at[step],
+            device_id=(1 - row, peer, inst),
+            device_id_type=MESH,
+        )
+        copy.start()
+        copies.append(copy)
     mine.wait()
     for copy in copies:
         copy.wait()
@@ -263,29 +269,25 @@
     smem = pl.BlockSpec(memory_space=pltpu.SMEM)
     hbm = pl.BlockSpec(memory_space=pl.ANY)
     packet = jax.ShapeDtypeStruct((sectors, inst_local * capacity * SLOT_ROWS, LANES), jnp.bfloat16)
-    send = pl.pallas_call(
-        functools.partial(gather_kernel, capacity),
-        out_shape=packet,
-        in_specs=[smem, smem, vmem, vmem, vmem],
-        out_specs=vmem,
-        scratch_shapes=[pltpu.VMEM((inst_local, SLOT_ROWS, cells), jnp.bfloat16)],
-        compiler_params=pltpu.CompilerParams(vmem_limit_bytes=VMEM_LIMIT),
-    )(block_count.reshape(1), matching[0, 0], donor_cells[0, 0], flow, gradients[0, 0])
     compact = flow.transpose(1, 0, 2)
     recv, everything = pl.pallas_call(
-        functools.partial(exchange_kernel, sectors, insts),
+        functools.partial(exchange_kernel, sectors, insts, capacity),
         out_shape=(packet, jax.ShapeDtypeStruct((insts,) + compact.shape, flow.dtype)),
-        in_specs=[hbm, hbm],
+        in_specs=[smem, smem, vmem, vmem, vmem, hbm],
         out_specs=(hbm, hbm),
         scratch_shapes=[
+            pltpu.VMEM((inst_local, SLOT_ROWS, cells), jnp.bfloat16),
+            pltpu.VMEM(packet.shape, packet.dtype),
             pltpu.SemaphoreType.DMA((sectors,)),
             pltpu.SemaphoreType.DMA((sectors,)),
             pltpu.SemaphoreType.DMA((insts - 1,)),
             pltpu.SemaphoreType.DMA((insts - 1,)),
             pltpu.SemaphoreType.DMA,
         ],
-        compiler_params=pltpu.CompilerParams(collective_id=0, has_side_effects=True),
-    )(send, compact)
+        compiler_params=pltpu.CompilerParams(
+            collective_id=0, has_side_effects=True, vmem_limit_bytes=VMEM_LIMIT
+        ),
+    )(block_count.reshape(1), matching[0, 0], donor_cells[0, 0], flow, gradients[0, 0], compact)
     dmat = jnp.asarray(spectral_matrix(inst_local * insts))
     result = pl.pallas_call(
         update_kernel,

time: 69.4 us -> 58.9 us (0.85)
  Pallas kernels: 60.6 us -> 51.9 us
  local copies, waits for them, and re-layouts: 7 us -> 5.23 us
    pallas_call x2 -> x1, Pallas kernels: 42.8 us -> 34.1 us  [body(): pl.pallas_call(functools.partial(exchange_kernel, sectors, insts, capacit...]
    unnamed x26 -> x20, local copies, waits for them, and re-layouts: 4.56 us -> 3.52 us
    transpose x1, local copies, waits for them, and re-layouts: 1.1 us -> 0.37 us  [body(): compact = flow.transpose(1, 0, 2)]
where the time goes in v3:
time: 58.9 us; the launch traced here: 58.6 us
  Pallas kernels  51.9 us (88%)
  local copies, waits for them, and re-layouts  5.23 us (9%)
  between operations  1.51 us (3%)
    pallas_call x1, Pallas kernels, body(): pl.pallas_call(functools.partial(exchange_kernel, sectors, insts, capacit...  34.1 us
    pallas_call x1, Pallas kernels, body(): pl.pallas_call(update_kernel, out_shape=jax.ShapeDtypeStruct(flow.shape,...  17.8 us
    unnamed x20, local copies, waits for them, and re-layouts  3.52 us
    broadcast_in_dim x1, local copies, waits for them, and re-layouts, body(): return result[None, None]  1.34 us

profile of v3, /device:TPU:9, one launch (start us, length us, event | category | flops | bytes accessed | tf_op | source)
XLA Modules:
  0.0 58.6 jit_solution(4627848725799791198)
XLA Ops:
  0.0 0.0 copy-start.7
  1.4 0.8 %copy.27 = f32[1,1,2,4,2,3,128]{6,5,4,3,2,1,0:T(4,128)S(1)} copy(f32[1,1,2,4,2,3,128]{6,4,5,3,2,1,0:T(2,128)} %param.22) | data formatting | bytes 49152 | tf_op args[10]
  2.1 1.2 %copy.26 = bf16[1,1,2,5,16384]{4,3,2,1,0:T(8,128)(2,1)S(1)} copy(bf16[1,1,2,5,16384]{4,2,3,1,0:T(2,128)(2,1)} %param.12) | data formatting | bytes 655360 | tf_op args[0]
  3.3 0.0 copy-start.3
  3.3 0.0 copy-start.5
  3.3 0.4 copy.15.state_ref
  3.7 0.0 copy-done.7
  3.7 0.0 copy-start.6
  3.7 0.5 copy.25
  4.3 0.0 copy-done.3
  4.3 0.0 copy-done.5
  4.3 34.1 %shard_map.118 = (bf16[4,128,128]{2,1,0:T(8,128)(2,1)S(1)}, bf16[4,5,2,16384]{3,2,1,0:T(2,128)(2,1)S(1)}) custom-call(s32[1]{0:T(128)} %bitcast.22.count_ref, s32[2,8]{1,0:T(2,128)S(1)} %bitcast.34, s32[8,128]{1,0:T(8,128)S(1)} %bitcast.33, bf16[2,5,16384]{2,1,0:T(8,128)(2,1)S(1)} %bitcast.25, bf16[2,15,16384]{2,1,0:T(8,128)(2,1)S(1)} %bitcast.27, ...), custom_call_target="tpu_custom_call" | custom-call | tf_op jit(solution)/shard_map/pallas_call | solution.py:273
  38.4 0.0 copy-done.6
  38.4 0.0 copy-start
  38.5 0.0 copy-start.1
  38.5 0.0 copy-start.2
  38.5 0.0 copy-start.4
  38.5 0.9 %copy.24 = bf16[1,1,2,25,16384]{4,3,2,1,0:T(8,128)(2,1)S(1)} copy(bf16[1,1,2,25,16384]{4,2,3,1,0:T(2,128)(2,1)S(1)} %copy-done.6) | data formatting | bytes 3276800 | tf_op args[2]
  39.4 0.1 copy-done
  39.5 0.0 copy-done.1
  39.5 0.0 copy-done.2
  39.5 0.0 copy-done.4
  39.5 17.8 %shard_map.119 = f32[2,5,16384]{2,1,0:T(8,128)S(1)} custom-call(f32[8,8]{1,0:T(8,128)S(1)} %copy-done.4, f32[1]{0:T(128)S(6)} %copy.28.freq_ref, bf16[4,128,128]{2,1,0:T(8,128)(2,1)S(1)} %get-tuple-element.7.recv_ref, bf16[2,4,2,128,128]{4,3,2,1,0:T(8,128)(2,1)S(1)} %bitcast.29, f32[2,4,2,3,128]{4,3,2,1,0:T(4,128)S(1)} %bitcast.30, ...), custom_call_target="tpu_custom_call" | custom-call | tf_op jit(solution)/shard_map/pallas_call | solution.py:292
  57.3 1.3 %copy.18 = f32[1,1,2,5,16384]{4,2,3,1,0:T(2,128)} copy(f32[1,1,2,5,16384]{4,3,2,1,0:T(8,128)S(1)} %bitcast.28) | data formatting | bytes 1310720 | tf_op jit(solution)/shard_map/broadcast_in_dim | solution.py:316
Async XLA Ops:
  0.0 3.7 %copy-start.7 = (bf16[1,1,2,15,16384]{4,2,3,1,0:T(2,128)(2,1)S(1)}, bf16[1,1,2,15,16384]{4,2,3,1,0:T(2,128)(2,1)}, u32[]{:S(2)}) copy-start(bf16[1,1,2,15,16384]{4,2,3,1,0:T(2,128)(2,1)} %param.13) | copy-start | bytes 2949124
  3.3 1.0 %copy-start.3 = (s32[1,1,8,128]{3,2,1,0:T(8,128)S(1)}, s32[1,1,8,128]{3,2,1,0:T(8,128)}, u32[]{:S(2)}) copy-start(s32[1,1,8,128]{3,2,1,0:T(8,128)} %param.17) | copy-start | bytes 12292
  3.3 1.0 %copy-start.5 = (s32[1,1,2,8]{3,2,1,0:T(2,128)S(1)}, s32[1,1,2,8]{3,2,1,0:T(2,128)}, u32[]{:S(2)}) copy-start(s32[1,1,2,8]{3,2,1,0:T(2,128)} %param.19) | copy-start | bytes 196
  3.7 34.7 %copy-start.6 = (bf16[1,1,2,25,16384]{4,2,3,1,0:T(2,128)(2,1)S(1)}, bf16[1,1,2,25,16384]{4,2,3,1,0:T(2,128)(2,1)}, u32[]{:S(2)}) copy-start(bf16[1,1,2,25,16384]{4,2,3,1,0:T(2,128)(2,1)} %param.14) | copy-start | bytes 4915204
  38.4 1.0 %copy-start = (bf16[1,1,2,4,2,128,128]{6,5,4,3,2,1,0:T(8,128)(2,1)S(1)}, bf16[1,1,2,4,2,128,128]{6,5,4,3,2,1,0:T(8,128)(2,1)}, u32[]{:S(2)}) copy-start(bf16[1,1,2,4,2,128,128]{6,5,4,3,2,1,0:T(8,128)(2,1)} %param.21) | copy-start | bytes 1572868
  38.5 1.1 %copy-start.1 = (f32[1,1,2,16384]{3,2,1,0:T(2,128)S(1)}, f32[1,1,2,16384]{3,2,1,0:T(2,128)}, u32[]{:S(2)}) copy-start(f32[1,1,2,16384]{3,2,1,0:T(2,128)} %param.15) | copy-start | bytes 393220
  38.5 1.0 %copy-start.2 = (s32[1,1,2,4,2,128]{5,4,3,2,1,0:T(2,128)S(1)}, s32[1,1,2,4,2,128]{5,4,3,2,1,0:T(2,128)}, u32[]{:S(2)}) copy-start(s32[1,1,2,4,2,128]{5,4,3,2,1,0:T(2,128)} %param.20) | copy-start | bytes 24580
  38.5 1.0 %copy-start.4 = (f32[8,8]{1,0:T(8,128)S(1)}, f32[8,8]{1,0:T(8,128)}, u32[]{:S(2)}) copy-start(f32[8,8]{1,0:T(8,128)} %constant.2.clone.dmat_ref) | copy-start | bytes 772

commit v4 on v3

--- a/solution.py
+++ b/solution.py
@@ -189,25 +189,27 @@
         lax.fori_loop(0, cells // WIDE // group, spread, 0)
 
     chunk = 8 * LANES
-    for t in range(inst_local):
-        coefs = [
-            [dmat_ref[first_row + t, i * inst_local + u] * rotation for u in range(inst_local)]
-            for i in range(insts)
-        ]
-
-        def relax(c, carry):
-            window = pl.ds(pl.multiple_of(c * chunk, chunk), chunk)
+    coefs = [
+        [dmat_ref[first_row + t, u] * rotation for u in range(insts * inst_local)]
+        for t in range(inst_local)
+    ]
+
+    def relax(c, carry):
+        window = pl.ds(pl.multiple_of(c * chunk, chunk), chunk)
+        position = lax.broadcasted_iota(jnp.int32, (inst_local, chunk), 0)
+        mixtures = [jnp.zeros((nvar, inst_local, chunk), jnp.float32)] * inst_local
+        for i in range(insts):
+            segment = all_ref[i, :, :, window].astype(jnp.float32)
+            for t in range(inst_local):
+                factor = jnp.zeros((inst_local, chunk), jnp.float32)
+                for u in range(inst_local):
+                    factor = jnp.where(position == u, coefs[t][i * inst_local + u], factor)
+                mixtures[t] = mixtures[t] + factor[None] * segment
+        for t in range(inst_local):
             jac = jac_ref[t, :, window].astype(jnp.float32)
             flow = state_ref[t, :, window].astype(jnp.float32)
             pseudo = pseudo_ref[t : t + 1, window]
-            position = lax.broadcasted_iota(jnp.int32, (inst_local, chunk), 0)
-            mixture = jnp.zeros((nvar, inst_local, chunk), jnp.float32)
-            for i in range(insts):
-                factor = jnp.zeros((inst_local, chunk), jnp.float32)
-                for u in range(inst_local):
-                    factor = jnp.where(position == u, coefs[i][u], factor)
-                mixture = mixture + factor[None] * all_ref[i, :, :, window].astype(jnp.float32)
-            rest = jnp.sum(mixture, axis=1) - coupling[t, 0:nvar, window]
+            rest = jnp.sum(mixtures[t], axis=1) - coupling[t, 0:nvar, window]
             for j in range(8):
                 lanes = slice(j * LANES, (j + 1) * LANES)
                 at = j * STAGE_ROWS
@@ -241,9 +243,9 @@
             for j in range(8):
                 begin = pl.multiple_of(c * chunk + j * LANES, LANES)
                 out_ref[t, :, pl.ds(begin, LANES)] = out_stage[j * 8 : j * 8 + nvar, :]
-            return carry
-
-        lax.fori_loop(0, cells // chunk, relax, 0)
+        return carry
+
+    lax.fori_loop(0, cells // chunk, relax, 0)
 
 
 def body(

time: 58.9 us -> 58.6 us (level)
  no operation moved by 1% of the time
where the time goes in v4:
time: 58.6 us; the launch traced here: 58.4 us
  Pallas kernels  51.6 us (88%)
  local copies, waits for them, and re-layouts  5.23 us (9%)
  between operations  1.51 us (3%)
    pallas_call x1, Pallas kernels, body(): pl.pallas_call(functools.partial(exchange_kernel, sectors, insts, capacit...  34.1 us
    pallas_call x1, Pallas kernels, body(): pl.pallas_call(update_kernel, out_shape=jax.ShapeDtypeStruct(flow.shape,...  17.5 us
    unnamed x20, local copies, waits for them, and re-layouts  3.52 us
    broadcast_in_dim x1, local copies, waits for them, and re-layouts, body(): return result[None, None]  1.34 us

profile of v4, /device:TPU:9, one launch (start us, length us, event | category | flops | bytes accessed | tf_op | source)
XLA Modules:
  0.0 58.4 jit_solution(3907294924452370220)
XLA Ops:
  0.0 0.0 copy-start.7
  1.4 0.8 %copy.27 = f32[1,1,2,4,2,3,128]{6,5,4,3,2,1,0:T(4,128)S(1)} copy(f32[1,1,2,4,2,3,128]{6,4,5,3,2,1,0:T(2,128)} %param.22) | data formatting | bytes 49152 | tf_op args[10]
  2.1 1.2 %copy.26 = bf16[1,1,2,5,16384]{4,3,2,1,0:T(8,128)(2,1)S(1)} copy(bf16[1,1,2,5,16384]{4,2,3,1,0:T(2,128)(2,1)} %param.12) | data formatting | bytes 655360 | tf_op args[0]
  3.3 0.0 copy-start.3
  3.3 0.0 copy-start.5
  3.3 0.4 copy.15.state_ref
  3.7 0.0 copy-done.7
  3.7 0.0 copy-start.6
  3.7 0.5 copy.25
  4.3 0.0 copy-done.3
  4.3 0.0 copy-done.5
  4.3 34.1 %shard_map.118 = (bf16[4,128,128]{2,1,0:T(8,128)(2,1)S(1)}, bf16[4,5,2,16384]{3,2,1,0:T(2,128)(2,1)S(1)}) custom-call(s32[1]{0:T(128)} %bitcast.22.count_ref, s32[2,8]{1,0:T(2,128)S(1)} %bitcast.34, s32[8,128]{1,0:T(8,128)S(1)} %bitcast.33, bf16[2,5,16384]{2,1,0:T(8,128)(2,1)S(1)} %bitcast.25, bf16[2,15,16384]{2,1,0:T(8,128)(2,1)S(1)} %bitcast.27, ...), custom_call_target="tpu_custom_call" | custom-call | tf_op jit(solution)/shard_map/pallas_call | solution.py:275
  38.4 0.0 copy-done.6
  38.4 0.0 copy-start
  38.5 0.0 copy-start.1
  38.5 0.0 copy-start.2
  38.5 0.0 copy-start.4
  38.5 0.9 %copy.24 = bf16[1,1,2,25,16384]{4,3,2,1,0:T(8,128)(2,1)S(1)} copy(bf16[1,1,2,25,16384]{4,2,3,1,0:T(2,128)(2,1)S(1)} %copy-done.6) | data formatting | bytes 3276800 | tf_op args[2]
  39.4 0.1 copy-done
  39.5 0.0 copy-done.1
  39.5 0.0 copy-done.2
  39.5 0.0 copy-done.4
  39.5 17.5 %shard_map.119 = f32[2,5,16384]{2,1,0:T(8,128)S(1)} custom-call(f32[8,8]{1,0:T(8,128)S(1)} %copy-done.4, f32[1]{0:T(128)S(6)} %copy.28.freq_ref, bf16[4,128,128]{2,1,0:T(8,128)(2,1)S(1)} %get-tuple-element.7.recv_ref, bf16[2,4,2,128,128]{4,3,2,1,0:T(8,128)(2,1)S(1)} %bitcast.29, f32[2,4,2,3,128]{4,3,2,1,0:T(4,128)S(1)} %bitcast.30, ...), custom_call_target="tpu_custom_call" | custom-call | tf_op jit(solution)/shard_map/pallas_call | solution.py:294
  57.0 1.3 %copy.18 = f32[1,1,2,5,16384]{4,2,3,1,0:T(2,128)} copy(f32[1,1,2,5,16384]{4,3,2,1,0:T(8,128)S(1)} %bitcast.28) | data formatting | bytes 1310720 | tf_op jit(solution)/shard_map/broadcast_in_dim | solution.py:318
Async XLA Ops:
  0.0 3.7 %copy-start.7 = (bf16[1,1,2,15,16384]{4,2,3,1,0:T(2,128)(2,1)S(1)}, bf16[1,1,2,15,16384]{4,2,3,1,0:T(2,128)(2,1)}, u32[]{:S(2)}) copy-start(bf16[1,1,2,15,16384]{4,2,3,1,0:T(2,128)(2,1)} %param.13) | copy-start | bytes 2949124
  3.3 1.0 %copy-start.3 = (s32[1,1,8,128]{3,2,1,0:T(8,128)S(1)}, s32[1,1,8,128]{3,2,1,0:T(8,128)}, u32[]{:S(2)}) copy-start(s32[1,1,8,128]{3,2,1,0:T(8,128)} %param.17) | copy-start | bytes 12292
  3.3 1.0 %copy-start.5 = (s32[1,1,2,8]{3,2,1,0:T(2,128)S(1)}, s32[1,1,2,8]{3,2,1,0:T(2,128)}, u32[]{:S(2)}) copy-start(s32[1,1,2,8]{3,2,1,0:T(2,128)} %param.19) | copy-start | bytes 196
  3.7 34.7 %copy-start.6 = (bf16[1,1,2,25,16384]{4,2,3,1,0:T(2,128)(2,1)S(1)}, bf16[1,1,2,25,16384]{4,2,3,1,0:T(2,128)(2,1)}, u32[]{:S(2)}) copy-start(bf16[1,1,2,25,16384]{4,2,3,1,0:T(2,128)(2,1)} %param.14) | copy-start | bytes 4915204
  38.4 1.0 %copy-start = (bf16[1,1,2,4,2,128,128]{6,5,4,3,2,1,0:T(8,128)(2,1)S(1)}, bf16[1,1,2,4,2,128,128]{6,5,4,3,2,1,0:T(8,128)(2,1)}, u32[]{:S(2)}) copy-start(bf16[1,1,2,4,2,128,128]{6,5,4,3,2,1,0:T(8,128)(2,1)} %param.21) | copy-start | bytes 1572868
  38.5 1.1 %copy-start.1 = (f32[1,1,2,16384]{3,2,1,0:T(2,128)S(1)}, f32[1,1,2,16384]{3,2,1,0:T(2,128)}, u32[]{:S(2)}) copy-start(f32[1,1,2,16384]{3,2,1,0:T(2,128)} %param.15) | copy-start | bytes 393220
  38.5 1.0 %copy-start.2 = (s32[1,1,2,4,2,128]{5,4,3,2,1,0:T(2,128)S(1)}, s32[1,1,2,4,2,128]{5,4,3,2,1,0:T(2,128)}, u32[]{:S(2)}) copy-start(s32[1,1,2,4,2,128]{5,4,3,2,1,0:T(2,128)} %param.20) | copy-start | bytes 24580
  38.5 1.0 %copy-start.4 = (f32[8,8]{1,0:T(8,128)S(1)}, f32[8,8]{1,0:T(8,128)}, u32[]{:S(2)}) copy-start(f32[8,8]{1,0:T(8,128)} %constant.2.clone.dmat_ref) | copy-start | bytes 772

commit v5 on v4

--- a/solution.py
+++ b/solution.py
@@ -84,9 +84,57 @@
                 )
 
 
+def couple_faces(nvar, recv_ref, weights_ref, offsets_ref, targets_ref, faces, coupling):
+    inst_local, sectors, capacity = targets_ref.shape[:3]
+    cells = coupling.shape[2]
+    faces[...] = jnp.zeros_like(faces)
+    group = 4
+    for t in range(inst_local):
+        target_rows = []
+        for m in range(sectors):
+            for k in range(capacity):
+                slot = t * capacity + k
+                column = (m * capacity + k) * LANES
+                mixed = jnp.dot(
+                    recv_ref[m, slot * SLOT_ROWS : (slot + 1) * SLOT_ROWS, :],
+                    weights_ref[t, m, k],
+                    preferred_element_type=jnp.float32,
+                )
+                value = mixed[0:nvar]
+                for d in range(3):
+                    begin = 16 + d * nvar
+                    value = value + offsets_ref[t, m, k, d : d + 1, :] * mixed[begin : begin + nvar]
+                upper = value.astype(jnp.bfloat16).astype(jnp.float32)
+                faces[t, 0:nvar, column : column + LANES] = upper
+                faces[t, 8 : 8 + nvar, column : column + LANES] = value - upper
+                target_rows.append(targets_ref[t, m, k : k + 1, :])
+        target_row = jnp.concatenate(target_rows, axis=1)
+        high = target_row >> 8
+        hot = one_hot_rows(target_row & (WIDE - 1))
+
+        def spread(g, carry):
+            face_values = faces[t]
+            rows = [jnp.where(high == g * group + j, face_values, 0.0) for j in range(group)]
+            placed = lax.dot_general(
+                jnp.concatenate(rows, axis=0).astype(jnp.bfloat16),
+                hot,
+                (((1,), (1,)), ((), ())),
+                preferred_element_type=jnp.float32,
+            )
+            for j in range(group):
+                begin = pl.multiple_of((g * group + j) * WIDE, WIDE)
+                coupling[t, :, pl.ds(begin, WIDE)] = (
+                    placed[j * 16 : j * 16 + 8] + placed[j * 16 + 8 : j * 16 + 16]
+                )
+            return carry
+
+        lax.fori_loop(0, cells // WIDE // group, spread, 0)
+
+
 def exchange_kernel(
-    sectors, insts, capacity, count_ref, matching_ref, donor_ref, flow_ref, grad_ref, state_ref,
-    recv_ref, all_ref, source, send_ref, fs, fr, ss, sr, own,
+    sectors, insts, capacity, count_ref, matching_ref, donor_ref, flow_ref, grad_ref, weights_ref,
+    offsets_ref, targets_ref, state_ref, coupling, all_ref, source, send_ref, recv_ref, faces,
+    fs, fr, ss, sr, own,
 ):
     row = lax.axis_index("row")
     sector = lax.axis_index("sector")
@@ -119,6 +167,7 @@
     gather_faces(
         capacity, count_ref, matching_ref, donor_ref, flow_ref, grad_ref, send_ref, source
     )
+    arrivals = []
     for step in range(sectors):
         peer = (sector + step) % sectors
         copy = pltpu.make_async_remote_copy(
@@ -130,64 +179,24 @@
             device_id_type=MESH,
         )
         copy.start()
-        copies.append(copy)
+        arrivals.append(copy)
+    for copy in arrivals:
+        copy.wait()
+    couple_faces(
+        flow_ref.shape[1], recv_ref, weights_ref, offsets_ref, targets_ref, faces, coupling
+    )
     mine.wait()
     for copy in copies:
         copy.wait()
 
 
 def update_kernel(
-    dmat_ref, freq_ref, recv_ref, weights_ref, offsets_ref, targets_ref, all_ref, state_ref,
-    jac_ref, pseudo_ref, out_ref, faces, coupling, stage, out_stage,
+    dmat_ref, freq_ref, coupling, all_ref, state_ref, jac_ref, pseudo_ref, out_ref, stage, out_stage
 ):
     inst_local, nvar, cells = state_ref.shape
-    sectors, capacity = targets_ref.shape[1:3]
     insts = all_ref.shape[0]
     first_row = lax.axis_index("inst") * inst_local
     rotation = freq_ref[0]
-    faces[...] = jnp.zeros_like(faces)
-    group = 4
-    for t in range(inst_local):
-        target_rows = []
-        for m in range(sectors):
-            for k in range(capacity):
-                slot = t * capacity + k
-                column = (m * capacity + k) * LANES
-                mixed = jnp.dot(
-                    recv_ref[m, slot * SLOT_ROWS : (slot + 1) * SLOT_ROWS, :],
-                    weights_ref[t, m, k],
-                    preferred_element_type=jnp.float32,
-                )
-                value = mixed[0:nvar]
-                for d in range(3):
-                    begin = 16 + d * nvar
-                    value = value + offsets_ref[t, m, k, d : d + 1, :] * mixed[begin : begin + nvar]
-                upper = value.astype(jnp.bfloat16).astype(jnp.float32)
-                faces[t, 0:nvar, column : column + LANES] = upper
-                faces[t, 8 : 8 + nvar, column : column + LANES] = value - upper
-                target_rows.append(targets_ref[t, m, k : k + 1, :])
-        target_row = jnp.concatenate(target_rows, axis=1)
-        high = target_row >> 8
-        hot = one_hot_rows(target_row & (WIDE - 1))
-
-        def spread(g, carry):
-            face_values = faces[t]
-            rows = [jnp.where(high == g * group + j, face_values, 0.0) for j in range(group)]
-            placed = lax.dot_general(
-                jnp.concatenate(rows, axis=0).astype(jnp.bfloat16),
-                hot,
-                (((1,), (1,)), ((), ())),
-                preferred_element_type=jnp.float32,
-            )
-            for j in range(group):
-                begin = pl.multiple_of((g * group + j) * WIDE, WIDE)
-                coupling[t, :, pl.ds(begin, WIDE)] = (
-                    placed[j * 16 : j * 16 + 8] + placed[j * 16 + 8 : j * 16 + 16]
-                )
-            return carry
-
-        lax.fori_loop(0, cells // WIDE // group, spread, 0)
-
     chunk = 8 * LANES
     coefs = [
         [dmat_ref[first_row + t, u] * rotation for u in range(insts * inst_local)]
@@ -272,14 +281,16 @@
     hbm = pl.BlockSpec(memory_space=pl.ANY)
     packet = jax.ShapeDtypeStruct((sectors, inst_local * capacity * SLOT_ROWS, LANES), jnp.bfloat16)
     compact = flow.transpose(1, 0, 2)
-    recv, everything = pl.pallas_call(
+    coupling, everything = pl.pallas_call(
         functools.partial(exchange_kernel, sectors, insts, capacity),
-        out_shape=(packet, jax.ShapeDtypeStruct((insts,) + compact.shape, flow.dtype)),
-        in_specs=[smem, smem, vmem, vmem, vmem, hbm],
-        out_specs=(hbm, hbm),
+        out_shape=(jax.ShapeDtypeStruct((inst_local, 8, cells), jnp.float32), jax.ShapeDtypeStruct((insts,) + compact.shape, flow.dtype)),
+        in_specs=[smem, smem] + [vmem] * 6 + [hbm],
+        out_specs=(vmem, hbm),
         scratch_shapes=[
             pltpu.VMEM((inst_local, SLOT_ROWS, cells), jnp.bfloat16),
             pltpu.VMEM(packet.shape, packet.dtype),
+            pltpu.VMEM(packet.shape, packet.dtype),
+            pltpu.VMEM((inst_local, 16, columns), jnp.float32),
             pltpu.SemaphoreType.DMA((sectors,)),
             pltpu.SemaphoreType.DMA((sectors,)),
             pltpu.SemaphoreType.DMA((insts - 1,)),
@@ -289,16 +300,15 @@
         compiler_params=pltpu.CompilerParams(
             collective_id=0, has_side_effects=True, vmem_limit_bytes=VMEM_LIMIT
         ),
-    )(block_count.reshape(1), matching[0, 0], donor_cells[0, 0], flow, gradients[0, 0], compact)
+    )(block_count.reshape(1), matching[0, 0], donor_cells[0, 0], flow, gradients[0, 0],
+      interp_weights[0, 0], face_offsets[0, 0], target_cells[0, 0], compact)
     dmat = jnp.asarray(spectral_matrix(inst_local * insts))
     result = pl.pallas_call(
         update_kernel,
         out_shape=jax.ShapeDtypeStruct(flow.shape, jnp.float32),
-        in_specs=[smem, smem] + [vmem] * 8,
+        in_specs=[smem, smem] + [vmem] * 5,
         out_specs=vmem,
         scratch_shapes=[
-            pltpu.VMEM((inst_local, 16, columns), jnp.float32),
-            pltpu.VMEM((inst_local, 8, cells), jnp.float32),
             pltpu.VMEM((8 * STAGE_ROWS, LANES), jnp.float32),
             pltpu.VMEM((64, LANES), jnp.float32),
         ],
@@ -306,10 +316,7 @@
     )(
         dmat,
         frequency,
-        recv,
-        interp_weights[0, 0],
-        face_offsets[0, 0],
-        target_cells[0, 0],
+        coupling,
         everything,
         flow,
         jacobian[0, 0],

time: 58.6 us -> 48.8 us (0.83)
  Pallas kernels: 51.6 us -> 41.9 us
    pallas_call x1, Pallas kernels: 17.5 us -> 7.79 us  [body(): pl.pallas_call(update_kernel, out_shape=jax.ShapeDtypeStruct(flow.shape,...]
where the time goes in v5:
time: 48.8 us; the launch traced here: 48.6 us
  Pallas kernels  41.9 us (86%)
  local copies, waits for them, and re-layouts  5.18 us (11%)
  between operations  1.51 us (3%)
    pallas_call x1, Pallas kernels, body(): pl.pallas_call(functools.partial(exchange_kernel, sectors, insts, capacit...  34.1 us
    pallas_call x1, Pallas kernels, body(): pl.pallas_call(update_kernel, out_shape=jax.ShapeDtypeStruct(flow.shape,...  7.79 us
    unnamed x20, local copies, waits for them, and re-layouts  3.47 us
    broadcast_in_dim x1, local copies, waits for them, and re-layouts, body(): return result[None, None]  1.34 us

profile of v5, /device:TPU:9, one launch (start us, length us, event | category | flops | bytes accessed | tf_op | source)
XLA Modules:
  0.0 48.6 jit_solution(6674872359832937439)
XLA Ops:
  0.0 0.0 copy-start.7
  1.4 0.8 %copy.27 = f32[1,1,2,4,2,3,128]{6,5,4,3,2,1,0:T(4,128)S(1)} copy(f32[1,1,2,4,2,3,128]{6,4,5,3,2,1,0:T(2,128)} %param.22) | data formatting | bytes 49152 | tf_op args[10]
  2.1 1.2 %copy.26 = bf16[1,1,2,5,16384]{4,3,2,1,0:T(8,128)(2,1)S(1)} copy(bf16[1,1,2,5,16384]{4,2,3,1,0:T(2,128)(2,1)} %param.12) | data formatting | bytes 655360 | tf_op args[0]
  3.3 0.0 copy-start
  3.3 0.0 copy-start.2
  3.3 0.0 copy-start.3
  3.3 0.0 copy-start.5
  3.4 0.4 copy.16.state_ref
  3.7 0.0 copy-done.7
  3.7 0.5 %copy.25 = bf16[1,1,2,15,16384]{4,3,2,1,0:T(8,128)(2,1)S(1)} copy(bf16[1,1,2,15,16384]{4,2,3,1,0:T(2,128)(2,1)S(1)} %copy-done.7) | data formatting | bytes 1966080 | tf_op args[1]
  4.3 0.0 copy-start.6
  4.3 0.0 copy-done
  4.4 0.0 copy-done.2
  4.4 0.0 copy-done.3
  4.4 0.0 copy-done.5
  4.4 34.1 %shard_map.118 = (f32[2,8,16384]{2,1,0:T(8,128)S(1)}, bf16[4,5,2,16384]{3,2,1,0:T(2,128)(2,1)S(1)}) custom-call(s32[1]{0:T(128)} %bitcast.22.count_ref, s32[2,8]{1,0:T(2,128)S(1)} %bitcast.34, s32[8,128]{1,0:T(8,128)S(1)} %bitcast.33, bf16[2,5,16384]{2,1,0:T(8,128)(2,1)S(1)} %bitcast.25, bf16[2,15,16384]{2,1,0:T(8,128)(2,1)S(1)} %bitcast.27, ...), custom_call_target="tpu_custom_call" | custom-call | tf_op jit(solution)/shard_map/pallas_call | solution.py:284
  38.5 0.0 copy-done.6
  38.5 0.0 copy-start.1
  38.5 0.0 copy-start.4
  38.5 0.9 %copy.24 = bf16[1,1,2,25,16384]{4,3,2,1,0:T(8,128)(2,1)S(1)} copy(bf16[1,1,2,25,16384]{4,2,3,1,0:T(2,128)(2,1)S(1)} %copy-done.6) | data formatting | bytes 3276800 | tf_op args[2]
  39.4 0.0 copy-done.1
  39.4 0.0 copy-done.4
  39.5 7.8 %shard_map.119 = f32[2,5,16384]{2,1,0:T(8,128)S(1)} custom-call(f32[8,8]{1,0:T(8,128)S(1)} %copy-done.4, f32[1]{0:T(128)S(6)} %copy.28.freq_ref, f32[2,8,16384]{2,1,0:T(8,128)S(1)} %get-tuple-element.7.coupling, bf16[4,5,2,16384]{3,2,1,0:T(2,128)(2,1)S(1)} %get-tuple-element.8.all_ref, bf16[2,5,16384]{2,1,0:T(8,128)(2,1)S(1)} %bitcast.26, ...), custom_call_target="tpu_custom_call" | custom-call | tf_op jit(solution)/shard_map/pallas_call | solution.py:306
  47.2 1.3 %copy.18 = f32[1,1,2,5,16384]{4,2,3,1,0:T(2,128)} copy(f32[1,1,2,5,16384]{4,3,2,1,0:T(8,128)S(1)} %bitcast.28) | data formatting | bytes 1310720 | tf_op jit(solution)/shard_map/broadcast_in_dim | solution.py:325
Async XLA Ops:
  0.0 3.7 %copy-start.7 = (bf16[1,1,2,15,16384]{4,2,3,1,0:T(2,128)(2,1)S(1)}, bf16[1,1,2,15,16384]{4,2,3,1,0:T(2,128)(2,1)}, u32[]{:S(2)}) copy-start(bf16[1,1,2,15,16384]{4,2,3,1,0:T(2,128)(2,1)} %param.13) | copy-start | bytes 2949124
  3.3 1.0 %copy-start = (bf16[1,1,2,4,2,128,128]{6,5,4,3,2,1,0:T(8,128)(2,1)S(1)}, bf16[1,1,2,4,2,128,128]{6,5,4,3,2,1,0:T(8,128)(2,1)}, u32[]{:S(2)}) copy-start(bf16[1,1,2,4,2,128,128]{6,5,4,3,2,1,0:T(8,128)(2,1)} %param.21) | copy-start | bytes 1572868
  3.3 1.0 %copy-start.2 = (s32[1,1,2,4,2,128]{5,4,3,2,1,0:T(2,128)S(1)}, s32[1,1,2,4,2,128]{5,4,3,2,1,0:T(2,128)}, u32[]{:S(2)}) copy-start(s32[1,1,2,4,2,128]{5,4,3,2,1,0:T(2,128)} %param.20) | copy-start | bytes 24580
  3.3 1.0 %copy-start.3 = (s32[1,1,8,128]{3,2,1,0:T(8,128)S(1)}, s32[1,1,8,128]{3,2,1,0:T(8,128)}, u32[]{:S(2)}) copy-start(s32[1,1,8,128]{3,2,1,0:T(8,128)} %param.17) | copy-start | bytes 12292
  3.3 1.0 %copy-start.5 = (s32[1,1,2,8]{3,2,1,0:T(2,128)S(1)}, s32[1,1,2,8]{3,2,1,0:T(2,128)}, u32[]{:S(2)}) copy-start(s32[1,1,2,8]{3,2,1,0:T(2,128)} %param.19) | copy-start | bytes 196
  4.3 34.2 %copy-start.6 = (bf16[1,1,2,25,16384]{4,2,3,1,0:T(2,128)(2,1)S(1)}, bf16[1,1,2,25,16384]{4,2,3,1,0:T(2,128)(2,1)}, u32[]{:S(2)}) copy-start(bf16[1,1,2,25,16384]{4,2,3,1,0:T(2,128)(2,1)} %param.14) | copy-start | bytes 4915204
  38.5 1.0 %copy-start.1 = (f32[1,1,2,16384]{3,2,1,0:T(2,128)S(1)}, f32[1,1,2,16384]{3,2,1,0:T(2,128)}, u32[]{:S(2)}) copy-start(f32[1,1,2,16384]{3,2,1,0:T(2,128)} %param.15) | copy-start | bytes 393220
  38.5 0.9 %copy-start.4 = (f32[8,8]{1,0:T(8,128)S(1)}, f32[8,8]{1,0:T(8,128)}, u32[]{:S(2)}) copy-start(f32[8,8]{1,0:T(8,128)} %constant.2.clone.dmat_ref) | copy-start | bytes 772

commit v6 on v5

--- a/solution.py
+++ b/solution.py
@@ -147,21 +147,32 @@
             barrier, inc=1, device_id=(row, sector, (inst + step) % insts), device_id_type=MESH
         )
     pl.semaphore_wait(barrier, sectors + insts - 1)
-    copies = []
-    for step in range(1, insts):
-        peer = (inst + step) % insts
-        copies.append(
-            pltpu.make_async_remote_copy(
-                src_ref=state_ref,
-                dst_ref=all_ref.at[inst],
-                send_sem=ss.at[step - 1],
-                recv_sem=sr.at[step - 1],
-                device_id=(row, sector, peer),
-                device_id_type=MESH,
-            )
+
+    def hop(side, step):
+        shift = 1 - 2 * side
+        origin = jnp.clip(inst - shift * step, 0, insts - 1)
+        slot = side * (insts - 1) + step
+        return pltpu.make_async_remote_copy(
+            src_ref=state_ref if step == 0 else all_ref.at[origin],
+            dst_ref=all_ref.at[origin],
+            send_sem=ss.at[slot],
+            recv_sem=sr.at[slot],
+            device_id=(row, sector, jnp.clip(inst + shift, 0, insts - 1)),
+            device_id_type=MESH,
         )
-    for copy in copies:
-        copy.start()
+
+    def behind(side):
+        return inst if side == 0 else insts - 1 - inst
+
+    def forward(step):
+        for side in range(2):
+            if step > 0:
+                pl.when(behind(side) >= step)(lambda: hop(side, step - 1).wait_recv())
+            if step < insts - 1:
+                sends = (behind(side) >= step) & (behind(side) < insts - 1)
+                pl.when(sends)(lambda: hop(side, step).start())
+
+    forward(0)
     mine = pltpu.make_async_copy(state_ref, all_ref.at[inst], own)
     mine.start()
     gather_faces(
@@ -180,14 +191,19 @@
         )
         copy.start()
         arrivals.append(copy)
+    forward(1)
     for copy in arrivals:
         copy.wait()
     couple_faces(
         flow_ref.shape[1], recv_ref, weights_ref, offsets_ref, targets_ref, faces, coupling
     )
     mine.wait()
-    for copy in copies:
-        copy.wait()
+    for step in range(2, insts):
+        forward(step)
+    for side in range(2):
+        for step in range(insts - 1):
+            sends = (behind(side) >= step) & (behind(side) < insts - 1)
+            pl.when(sends)(lambda: hop(side, step).wait_send())
 
 
 def update_kernel(
@@ -293,8 +309,8 @@
             pltpu.VMEM((inst_local, 16, columns), jnp.float32),
             pltpu.SemaphoreType.DMA((sectors,)),
             pltpu.SemaphoreType.DMA((sectors,)),
-            pltpu.SemaphoreType.DMA((insts - 1,)),
-            pltpu.SemaphoreType.DMA((insts - 1,)),
+            pltpu.SemaphoreType.DMA((2 * (insts - 1),)),
+            pltpu.SemaphoreType.DMA((2 * (insts - 1),)),
             pltpu.SemaphoreType.DMA,
         ],
         compiler_params=pltpu.CompilerParams(

time: 48.8 us -> 51 us (1.045)
  the two profiles are of different devices: /device:TPU:9 before, /device:TPU:0 now
where the time goes in v6:
time: 51 us; the launch traced here: 50.8 us
  Pallas kernels  44.1 us (86%)
  local copies, waits for them, and re-layouts  5.18 us (10%)
  between operations  1.51 us (3%)
    pallas_call x1, Pallas kernels, body(): pl.pallas_call(functools.partial(exchange_kernel, sectors, insts, capacit...  36.3 us
    pallas_call x1, Pallas kernels, body(): pl.pallas_call(update_kernel, out_shape=jax.ShapeDtypeStruct(flow.shape,...  7.79 us
    unnamed x20, local copies, waits for them, and re-layouts  3.47 us
    broadcast_in_dim x1, local copies, waits for them, and re-layouts, body(): return result[None, None]  1.34 us

profile of v6, /device:TPU:0, one launch (start us, length us, event | category | flops | bytes accessed | tf_op | source)
XLA Modules:
  0.0 50.8 jit_solution(11763386642507644130)
XLA Ops:
  0.0 0.0 copy-start.7
  1.4 0.8 %copy.27 = f32[1,1,2,4,2,3,128]{6,5,4,3,2,1,0:T(4,128)S(1)} copy(f32[1,1,2,4,2,3,128]{6,4,5,3,2,1,0:T(2,128)} %param.22) | data formatting | bytes 49152 | tf_op args[10]
  2.1 1.2 %copy.26 = bf16[1,1,2,5,16384]{4,3,2,1,0:T(8,128)(2,1)S(1)} copy(bf16[1,1,2,5,16384]{4,2,3,1,0:T(2,128)(2,1)} %param.12) | data formatting | bytes 655360 | tf_op args[0]
  3.3 0.0 copy-start
  3.3 0.0 copy-start.2
  3.3 0.0 copy-start.3
  3.3 0.0 copy-start.5
  3.4 0.4 copy.16.state_ref
  3.7 0.0 copy-done.7
  3.7 0.5 %copy.25 = bf16[1,1,2,15,16384]{4,3,2,1,0:T(8,128)(2,1)S(1)} copy(bf16[1,1,2,15,16384]{4,2,3,1,0:T(2,128)(2,1)S(1)} %copy-done.7) | data formatting | bytes 1966080 | tf_op args[1]
  4.3 0.0 copy-start.6
  4.3 0.0 copy-done
  4.4 0.0 copy-done.2
  4.4 0.0 copy-done.3
  4.4 0.0 copy-done.5
  4.4 36.3 %shard_map.118 = (f32[2,8,16384]{2,1,0:T(8,128)S(1)}, bf16[4,5,2,16384]{3,2,1,0:T(2,128)(2,1)S(1)}) custom-call(s32[1]{0:T(128)} %bitcast.22.count_ref, s32[2,8]{1,0:T(2,128)S(1)} %bitcast.34, s32[8,128]{1,0:T(8,128)S(1)} %bitcast.33, bf16[2,5,16384]{2,1,0:T(8,128)(2,1)S(1)} %bitcast.25, bf16[2,15,16384]{2,1,0:T(8,128)(2,1)S(1)} %bitcast.27, ...), custom_call_target="tpu_custom_call" | custom-call | tf_op jit(solution)/shard_map/pallas_call | solution.py:300
  40.6 0.0 copy-done.6
  40.7 0.0 copy-start.1
  40.7 0.0 copy-start.4
  40.7 0.9 %copy.24 = bf16[1,1,2,25,16384]{4,3,2,1,0:T(8,128)(2,1)S(1)} copy(bf16[1,1,2,25,16384]{4,2,3,1,0:T(2,128)(2,1)S(1)} %copy-done.6) | data formatting | bytes 3276800 | tf_op args[2]
  41.6 0.0 copy-done.1
  41.6 0.0 copy-done.4
  41.6 7.8 %shard_map.119 = f32[2,5,16384]{2,1,0:T(8,128)S(1)} custom-call(f32[8,8]{1,0:T(8,128)S(1)} %copy-done.4, f32[1]{0:T(128)S(6)} %copy.28.freq_ref, f32[2,8,16384]{2,1,0:T(8,128)S(1)} %get-tuple-element.7.coupling, bf16[4,5,2,16384]{3,2,1,0:T(2,128)(2,1)S(1)} %get-tuple-element.8.all_ref, bf16[2,5,16384]{2,1,0:T(8,128)(2,1)S(1)} %bitcast.26, ...), custom_call_target="tpu_custom_call" | custom-call | tf_op jit(solution)/shard_map/pallas_call | solution.py:322
  49.4 1.3 %copy.18 = f32[1,1,2,5,16384]{4,2,3,1,0:T(2,128)} copy(f32[1,1,2,5,16384]{4,3,2,1,0:T(8,128)S(1)} %bitcast.28) | data formatting | bytes 1310720 | tf_op jit(solution)/shard_map/broadcast_in_dim | solution.py:341
Async XLA Ops:
  0.0 3.7 %copy-start.7 = (bf16[1,1,2,15,16384]{4,2,3,1,0:T(2,128)(2,1)S(1)}, bf16[1,1,2,15,16384]{4,2,3,1,0:T(2,128)(2,1)}, u32[]{:S(2)}) copy-start(bf16[1,1,2,15,16384]{4,2,3,1,0:T(2,128)(2,1)} %param.13) | copy-start | bytes 2949124
  3.3 1.0 %copy-start = (bf16[1,1,2,4,2,128,128]{6,5,4,3,2,1,0:T(8,128)(2,1)S(1)}, bf16[1,1,2,4,2,128,128]{6,5,4,3,2,1,0:T(8,128)(2,1)}, u32[]{:S(2)}) copy-start(bf16[1,1,2,4,2,128,128]{6,5,4,3,2,1,0:T(8,128)(2,1)} %param.21) | copy-start | bytes 1572868
  3.3 1.0 %copy-start.2 = (s32[1,1,2,4,2,128]{5,4,3,2,1,0:T(2,128)S(1)}, s32[1,1,2,4,2,128]{5,4,3,2,1,0:T(2,128)}, u32[]{:S(2)}) copy-start(s32[1,1,2,4,2,128]{5,4,3,2,1,0:T(2,128)} %param.20) | copy-start | bytes 24580
  3.3 1.0 %copy-start.3 = (s32[1,1,8,128]{3,2,1,0:T(8,128)S(1)}, s32[1,1,8,128]{3,2,1,0:T(8,128)}, u32[]{:S(2)}) copy-start(s32[1,1,8,128]{3,2,1,0:T(8,128)} %param.17) | copy-start | bytes 12292
  3.3 1.0 %copy-start.5 = (s32[1,1,2,8]{3,2,1,0:T(2,128)S(1)}, s32[1,1,2,8]{3,2,1,0:T(2,128)}, u32[]{:S(2)}) copy-start(s32[1,1,2,8]{3,2,1,0:T(2,128)} %param.19) | copy-start | bytes 196
  4.3 36.4 %copy-start.6 = (bf16[1,1,2,25,16384]{4,2,3,1,0:T(2,128)(2,1)S(1)}, bf16[1,1,2,25,16384]{4,2,3,1,0:T(2,128)(2,1)}, u32[]{:S(2)}) copy-start(bf16[1,1,2,25,16384]{4,2,3,1,0:T(2,128)(2,1)} %param.14) | copy-start | bytes 4915204
  40.7 1.0 %copy-start.1 = (f32[1,1,2,16384]{3,2,1,0:T(2,128)S(1)}, f32[1,1,2,16384]{3,2,1,0:T(2,128)}, u32[]{:S(2)}) copy-start(f32[1,1,2,16384]{3,2,1,0:T(2,128)} %param.15) | copy-start | bytes 393220
  40.7 0.9 %copy-start.4 = (f32[8,8]{1,0:T(8,128)S(1)}, f32[8,8]{1,0:T(8,128)}, u32[]{:S(2)}) copy-start(f32[8,8]{1,0:T(8,128)} %constant.2.clone.dmat_ref) | copy-start | bytes 772
